TPU v7x, 512 devices: a whole 4x8x8 slice. The times are simulated.
512 devices in a mesh: section: 8 (over y), tp: 8 (over z), ctx: 8 (over x, core).
Axes of the slice: x: 4, y: 8, z: 8, core: 2. Of those that a mesh axis runs over, the one named last changes fastest.
Arguments:
- hidden: bfloat16 [32, 4096], P('section', 'ctx'), may hold values from -60 to 60
- gain: float32 [8, 4096], P('section', 'ctx'), may hold values from 0.1 to 1.9
- w_query: bfloat16 [8, 4096, 4096], P('section', 'ctx', 'tp'), may hold values from -0.09375 to 0.09375
- key_weight: bfloat16 [8, 4096, 1024], P('section', 'ctx', 'tp'), may hold values from -0.09375 to 0.09375
- value_weight: bfloat16 [8, 4096, 1024], P('section', 'ctx', 'tp'), may hold values from -0.09375 to 0.09375
- w_out: bfloat16 [8, 4096, 4096], P('section', ('tp', 'ctx')), may hold values from -1.5 to 1.5
- key_cache_slots: bfloat16 [32, 8192, 1024], P('section', 'ctx', 'tp'), may hold values from -64 to 64
- value_cache_slots: bfloat16 [32, 8192, 1024], P('section', 'ctx', 'tp'), may hold values from -6 to 6
- lengths: int32 [32], P('section'), may hold values from 1024 to 8192, as said below
- plan: int32 [32, 8, 2], P('section', 'ctx'), may hold values from 0 to 8192, as said below
- routing: int32 [8, 4], P('section'), may hold values from 0 to 3, each once within a row
Outputs:
- handed: bfloat16 [32, 4096], P('section', 'ctx')
- attn_out: float32 [32, 4096], P('section', 'ctx')
Inputs may be any that keep to these rules, and one draw needn't show every extreme that they name: `lengths`: in every section one request has the longest context, 8192. `plan`: for each request the spans [start, end) of the ctx indices follow one another in index order from 0 to the request's length; each holds at most 1024 positions, and some request of every section holds 1024 on every index. Slot j of span c holds position start + j; slots at or past end - start are not in the context. `routing`: each section's row names every row of the previous section's block once.
All inputs are finite; a program needn't handle non-finite values.
Results may differ from a plain program's by a relative error of at most 0.009.
Values may be sent and summed in bfloat16 or wider, within the bound.
No kernel may reach another device: no remote copies, remote signals or barrier semaphores. Data moves between devices by JAX's collectives and lax.ppermute only.
A program may use at most 64 MiB of HBM per device.

v0:
```python
import jax
import jax.numpy as jnp
from jax import lax
from jax.sharding import PartitionSpec as P

HEAD_SIZE = 128


EPSILON = 1e-05
NEGATIVE = -1e30
ROPE_BASE = 500000.0


def from_behind(value, axis, steps):
    count = lax.axis_size(axis)
    pairs = [(source, (source + steps) % count) for source in range(count)]
    return lax.ppermute(value, axis, pairs)


def apply_rotary(values, position):
    half_dim = values.shape[-1] // 2
    frequency = ROPE_BASE ** (-2.0 * jnp.arange(half_dim, dtype=jnp.float32) / values.shape[-1])
    angles = position.astype(jnp.float32)[:, None, None] * frequency
    cosine = jnp.cos(angles)
    sine_value = jnp.sin(angles)
    lower_half = values[..., :half_dim]
    upper_half = values[..., half_dim:]
    return jnp.concatenate(
        [
            lower_half * cosine - upper_half * sine_value,
            upper_half * cosine + lower_half * sine_value,
        ],
        axis=-1,
    )


def per_device(
    hidden,
    gain,
    w_query,
    key_weight,
    value_weight,
    w_out,
    key_cache_slots,
    value_cache_slots,
    lengths,
    plan,
    routing,
):
    request_count = hidden.shape[0]
    model_width = hidden.shape[1] * lax.axis_size("ctx")
    hidden_f = hidden.astype(jnp.float32)
    scaled_in = (hidden_f * gain[0]).astype(jnp.bfloat16)
    squares = jnp.sum(hidden_f * hidden_f, axis=1)
    query_part = jnp.dot(scaled_in, w_query[0], preferred_element_type=jnp.float32)
    key_part = jnp.dot(scaled_in, key_weight[0], preferred_element_type=jnp.float32)
    value_part = jnp.dot(scaled_in, value_weight[0], preferred_element_type=jnp.float32)
    squares, query_part, key_part, value_part = lax.psum(
        (squares, query_part, key_part, value_part), "ctx"
    )
    inverse = lax.rsqrt(squares / model_width + EPSILON)[:, None]
    kv_heads = key_part.shape[1] // HEAD_SIZE
    query_heads = query_part.shape[1] // HEAD_SIZE
    group_count = query_heads // kv_heads
    rotated_query = apply_rotary(
        (query_part * inverse).reshape(request_count, query_heads, HEAD_SIZE), lengths
    ).astype(jnp.bfloat16)
    fresh_key = apply_rotary(
        (key_part * inverse).reshape(request_count, kv_heads, HEAD_SIZE), lengths
    ).astype(jnp.bfloat16)
    fresh_value = (
        (value_part * inverse).reshape(request_count, kv_heads, HEAD_SIZE).astype(jnp.bfloat16)
    )
    query_by_group = rotated_query.reshape(request_count, kv_heads, group_count, HEAD_SIZE)
    slot_count = key_cache_slots.shape[1]
    stored_keys = key_cache_slots.reshape(request_count, slot_count, kv_heads, HEAD_SIZE)
    stored_values = value_cache_slots.reshape(request_count, slot_count, kv_heads, HEAD_SIZE)
    scores = jnp.einsum(
        "rkgd,rjkd->rkgj", query_by_group, stored_keys, preferred_element_type=jnp.float32
    ) * HEAD_SIZE ** (-0.5)
    counts = plan[:, 0, 1] - plan[:, 0, 0]
    live_slot = (jnp.arange(slot_count, dtype=jnp.int32)[None, :] < counts[:, None])[
        :, None, None, :
    ]
    masked = jnp.where(live_slot, scores, NEGATIVE)
    block_max = jnp.max(masked, axis=-1)
    weights = jnp.where(live_slot, jnp.exp(masked - block_max[..., None]), 0.0)
    block_sum = jnp.sum(weights, axis=-1)
    block_out = jnp.einsum(
        "rkgj,rjkd->rkgd",
        weights.astype(jnp.bfloat16),
        stored_values,
        preferred_element_type=jnp.float32,
    )
    top_score = lax.pmax(block_max, "ctx")
    factor = jnp.exp(block_max - top_score)
    total_sum, merged = lax.psum((block_sum * factor, block_out * factor[..., None]), "ctx")
    new_score = jnp.einsum(
        "rkgd,rkd->rkg", query_by_group, fresh_key, preferred_element_type=jnp.float32
    ) * HEAD_SIZE ** (-0.5)
    peak = jnp.maximum(top_score, new_score)
    old_factor = jnp.exp(top_score - peak)
    new_factor = jnp.exp(new_score - peak)
    total_sum = total_sum * old_factor + new_factor
    merged = (
        merged * old_factor[..., None]
        + new_factor[..., None] * fresh_value.astype(jnp.float32)[:, :, None, :]
    )
    attended = (
        (merged / total_sum[..., None])
        .astype(jnp.bfloat16)
        .reshape(request_count, query_heads * HEAD_SIZE)
    )
    column_width = attended.shape[1] // lax.axis_size("ctx")
    own_columns = lax.dynamic_slice_in_dim(
        attended, lax.axis_index("ctx") * column_width, column_width, 1
    )
    partial_out = jnp.dot(own_columns, w_out[0], preferred_element_type=jnp.float32)
    width_dev = hidden.shape[1]
    summed_all = lax.psum(partial_out, ("tp", "ctx"))
    branch_out = lax.dynamic_slice_in_dim(
        summed_all, lax.axis_index("ctx") * width_dev, width_dev, 1
    )
    section_rows = (hidden_f + branch_out).astype(jnp.bfloat16)
    arrived = from_behind(section_rows, "section", 1)
    selector = (routing[0][:, None] == jnp.arange(request_count, dtype=jnp.int32)[None, :]).astype(
        jnp.bfloat16
    )
    handed = jnp.dot(selector, arrived, preferred_element_type=jnp.float32).astype(jnp.bfloat16)
    return (handed, branch_out)


def solution(mesh):
    return jax.shard_map(
        per_device,
        mesh=mesh,
        in_specs=(
            P("section", "ctx"),
            P("section", "ctx"),
            P("section", "ctx", "tp"),
            P("section", "ctx", "tp"),
            P("section", "ctx", "tp"),
            P("section", ("tp", "ctx"), None),
            P("section", "ctx", "tp"),
            P("section", "ctx", "tp"),
            P("section"),
            P("section", "ctx", None),
            P("section", None),
        ),
        out_specs=(P("section", "ctx"), P("section", "ctx")),
        check_vma=False,
    )
```

profile of v0, /device:TPU:1, one launch (start us, length us, event | category | flops | bytes accessed | tf_op | source)
XLA Modules:
  0.0 263.6 jit_solution(10790133681905115837)
XLA Ops:
  7.2 0.0 copy-start
  7.2 0.0 all-reduce.4.cloned.1.call-start
  7.3 0.7 convert_element_type.42
  8.0 0.8 subtract_bitcast_fusion
  8.8 0.8 fusion.17
  9.6 0.0 copy-start.4
  9.6 0.0 copy-start.5
  9.6 1.2 fusion.8
  10.8 0.1 fusion.6
  10.9 0.1 iota_compare_fusion
  11.0 1.2 fusion.4
  12.2 19.1 %all-reduce.1 = (f32[4,512]{1,0:T(4,128)S(1)}, f32[4]{0:T(128)S(1)}) all-reduce(f32[4,512]{1,0:T(4,128)S(1)} %fusion.4, f32[4]{0:T(128)S(1)} %fusion.17), channel_id=1, replica_groups=mesh['section'=8,'tp'=8,'ctx'=8] {'ctx'}, use_global_device_ids=true, to_apply=%region_0.0 | all-reduce | flops 2052 | bytes 16416 | tf_op jit(solution)/shard_map/psum | solution.py:58
  31.3 0.1 broadcast_multiply_fusion
  31.3 0.1 multiply_cosine_fusion.1
  31.5 0.1 subtract_convert_fusion
  31.5 0.5 fusion.46
  32.0 12.5 %pmax.7 = f32[4,1,4]{2,0,1:T(4,128)S(1)} all-reduce(f32[4,1,4]{2,0,1:T(4,128)S(1)} %bitcast.62), channel_id=1, replica_groups=mesh['section'=8,'tp'=8,'ctx'=8] {'ctx'}, use_global_device_ids=true, to_apply=%region_4.0 | all-reduce | flops 16 | bytes 128 | tf_op jit(solution)/shard_map/pmax | solution.py:95
  44.5 0.2 fusion.10
  44.7 0.3 fusion.1
  45.0 20.7 %all-reduce = (f32[4,1,4]{2,0,1:T(4,128)S(1)}, f32[4,128]{1,0:T(4,128)S(1)}, f32[4,128]{1,0:T(4,128)S(1)}, f32[4,1,4,128]{3,2,0,1:T(4,128)S(1)}) all-reduce(f32[4,1,4]{2,0,1:T(4,128)S(1)} %get-tuple-element.16, f32[4,128]{1,0:T(4,128)S(1)} %fusion.8, f32[4,128]{1,0:T(4,128)S(1)} %fusion.6, ...), channel_id=1, replica_groups=mesh['section'=8,'tp'=8,'ctx'=8] {'ctx'}, use_global_device_ids=true, to_apply=%region_9.10 | all-reduce | flops 3088 | bytes 24704 | tf_op jit(solution)/shard_map/psum | solution.py:97
  65.7 0.1 fusion.33
  65.8 0.1 fusion.37
  65.9 0.1 maximum_bitcast_fusion
  66.0 0.2 fusion.31
  66.2 0.1 fusion.20
  66.3 0.9 fusion.2
  67.2 0.0 all-reduce.4.cloned.1.call-update
  67.2 181.7 %all-reduce.4.cloned.1.call-done = f32[4,4096]{1,0:T(4,128)} async-done(((f32[4,4096]{1,0:T(4,128)}), f32[4,4096]{1,0:T(4,128)}) %all-reduce.4.cloned.1.call-update) | async-done | bytes 65552 | tf_op jit(solution)/shard_map/psum | solution.py:120
  248.9 1.3 fusion.18
  250.2 3.2 %collective-permute-start = (bf16[4,512]{1,0:T(4,128)(2,1)S(1)}, bf16[4,512]{1,0:T(4,128)(2,1)S(1)}, u32[]{:S(2)}, u32[]{:S(2)}) collective-permute-start(bf16[4,512]{1,0:T(4,128)(2,1)S(1)} %get-tuple-element.8), channel_id=1, source_target_pairs={{0,64},{64,128},{128,192},{192,256},{256,320},{320,384},{384,448},... | collective-permute-start | bytes 12296 | tf_op jit(solution)/shard_map/ppermute | solution.py:17
  253.5 2.4 collective-permute-done
  255.9 0.8 convolution_convert_fusion
  (17 shorter events, 0.1 us)
Async XLA Ops:
  7.2 24.4 %copy-start = (bf16[4,1024,128]{2,1,0:T(8,128)(2,1)S(1)}, bf16[4,1024,128]{2,1,0:T(8,128)(2,1)}, u32[]{:S(2)}) copy-start(bf16[4,1024,128]{2,1,0:T(8,128)(2,1)} %param.17) | copy-start | bytes 3145732
  7.2 3.6 %copy-start.2 = (bf16[1,512,128]{2,1,0:T(8,128)(2,1)S(1)}, bf16[1,512,128]{2,1,0:T(8,128)(2,1)}, u32[]{:S(2)}) copy-start(bf16[1,512,128]{2,1,0:T(8,128)(2,1)} %param.15) | copy-start | bytes 393220
  7.2 241.8 %all-reduce.4.cloned.1.call-start = ((), (), s32[]{:S(2)}) async-start(), calls=%async_computation | async-start | bytes 131072 | tf_op jit(solution)/shard_map/psum | solution.py:120
  9.6 1.2 copy-start.3
  9.6 1.2 copy-start.4
  9.6 35.1 %copy-start.5 = (bf16[4,1024,128]{2,1,0:T(8,128)(2,1)S(1)}, bf16[4,1024,128]{2,1,0:T(8,128)(2,1)}, u32[]{:S(2)}) copy-start(bf16[4,1024,128]{2,1,0:T(8,128)(2,1)} %param.18) | copy-start | bytes 3145732
  44.7 21.6 %copy-start.1 = (bf16[1,64,4096]{2,1,0:T(8,128)(2,1)S(1)}, bf16[1,64,4096]{2,1,0:T(8,128)(2,1)}, u32[]{:S(2)}) copy-start(bf16[1,64,4096]{2,1,0:T(8,128)(2,1)} %param.16) | copy-start | bytes 1572868
  250.2 5.7 %copy-start.6 = (s32[1,4]{1,0:T(1,128)S(1)}, s32[1,4]{1,0:T(1,128)}, u32[]{:S(2)}) copy-start(s32[1,4]{1,0:T(1,128)} %param.21) | copy-start | bytes 52
  250.2 5.7 %collective-permute-start = (bf16[4,512]{1,0:T(4,128)(2,1)S(1)}, bf16[4,512]{1,0:T(4,128)(2,1)S(1)}, u32[]{:S(2)}, u32[]{:S(2)}) collective-permute-start(bf16[4,512]{1,0:T(4,128)(2,1)S(1)} %get-tuple-element.8), channel_id=1, source_target_pairs={{0,64},{64,128},{128,192},{192,256},{256,320},{320,384},{384,448},... | collective-permute-start | bytes 12296 | tf_op jit(solution)/shard_map/ppermute | solution.py:17
Sparse Core Ops, SparseCore 0:
  67.3 181.5 all-reduce.3
where the time goes:
time: 264 us
  waiting for transfers between devices  184 us (70%)
  blocking collectives  52.2 us (20%)
  between operations  14.2 us (5%)
  matrix products  5.15 us (2%)
  other arithmetic  4.5 us (2%)
  starting transfers between devices  3.27 us (1%)
    psum x1, waiting for transfers between devices, per_device(): summed_all = lax.psum(partial_out, ('tp', 'ctx'))  182 us
    psum x1, blocking collectives, per_device(): lax.psum((block_sum * factor, block_out * factor[..., None]), 'ctx')  20.7 us
    psum x1, blocking collectives, per_device(): lax.psum((squares, query_part, key_part, value_part), 'ctx')  19.1 us
    pmax x1, blocking collectives, per_device(): top_score = lax.pmax(block_max, 'ctx')  12.5 us
  transfers between devices with their start and end apart: 2, of which 2 were waited for; matrix products, arithmetic and copies ran while one was open for 0% of the time, Pallas kernels for 0%

commit v1 on v0

--- a/solution.py
+++ b/solution.py
@@ -15,6 +15,11 @@
     count = lax.axis_size(axis)
     pairs = [(source, (source + steps) % count) for source in range(count)]
     return lax.ppermute(value, axis, pairs)
+
+
+def spread(value, axis):
+    copies = jnp.broadcast_to(value[None], (lax.axis_size(axis),) + value.shape)
+    return lax.all_to_all(copies, axis, 0, 0, tiled=True)
 
 
 def apply_rotary(values, position):
@@ -55,9 +60,13 @@
     query_part = jnp.dot(scaled_in, w_query[0], preferred_element_type=jnp.float32)
     key_part = jnp.dot(scaled_in, key_weight[0], preferred_element_type=jnp.float32)
     value_part = jnp.dot(scaled_in, value_weight[0], preferred_element_type=jnp.float32)
-    squares, query_part, key_part, value_part = lax.psum(
-        (squares, query_part, key_part, value_part), "ctx"
-    )
+    packed = jnp.concatenate([query_part, key_part, value_part, squares[:, None]], axis=1)
+    packed = spread(packed, "ctx").sum(axis=0)
+    query_width, key_width = query_part.shape[1], key_part.shape[1]
+    query_part = packed[:, :query_width]
+    key_part = packed[:, query_width : query_width + key_width]
+    value_part = packed[:, query_width + key_width : query_width + 2 * key_width]
+    squares = packed[:, query_width + 2 * key_width]
     inverse = lax.rsqrt(squares / model_width + EPSILON)[:, None]
     kv_heads = key_part.shape[1] // HEAD_SIZE
     query_heads = query_part.shape[1] // HEAD_SIZE
@@ -92,35 +101,49 @@
         stored_values,
         preferred_element_type=jnp.float32,
     )
-    top_score = lax.pmax(block_max, "ctx")
-    factor = jnp.exp(block_max - top_score)
-    total_sum, merged = lax.psum((block_sum * factor, block_out * factor[..., None]), "ctx")
     new_score = jnp.einsum(
         "rkgd,rkd->rkg", query_by_group, fresh_key, preferred_element_type=jnp.float32
     ) * HEAD_SIZE ** (-0.5)
-    peak = jnp.maximum(top_score, new_score)
-    old_factor = jnp.exp(top_score - peak)
-    new_factor = jnp.exp(new_score - peak)
-    total_sum = total_sum * old_factor + new_factor
-    merged = (
-        merged * old_factor[..., None]
-        + new_factor[..., None] * fresh_value.astype(jnp.float32)[:, :, None, :]
-    )
-    attended = (
-        (merged / total_sum[..., None])
-        .astype(jnp.bfloat16)
-        .reshape(request_count, query_heads * HEAD_SIZE)
-    )
-    column_width = attended.shape[1] // lax.axis_size("ctx")
-    own_columns = lax.dynamic_slice_in_dim(
-        attended, lax.axis_index("ctx") * column_width, column_width, 1
-    )
+    ctx_count, ctx_index = lax.axis_size("ctx"), lax.axis_index("ctx")
+    column_width = query_heads * HEAD_SIZE // ctx_count
+    parts_per_head = HEAD_SIZE // column_width
+
+    def by_owner(per_head):
+        flat = per_head.reshape(request_count, query_heads)
+        return jnp.repeat(flat, parts_per_head, axis=1).T[:, :, None]
+
+    pieces = block_out.reshape(request_count, ctx_count, column_width).transpose(1, 0, 2)
+    packed = jnp.concatenate([pieces, by_owner(block_max), by_owner(block_sum)], axis=2)
+    packed = lax.all_to_all(packed, "ctx", 0, 0, tiled=True)
+    span_out = packed[:, :, :column_width]
+    span_max = packed[:, :, column_width]
+    span_sum = packed[:, :, column_width + 1]
+    own_score = lax.dynamic_index_in_dim(by_owner(new_score), ctx_index, 0, keepdims=False)[:, 0]
+    own_value = lax.dynamic_slice_in_dim(
+        fresh_value.reshape(request_count, HEAD_SIZE),
+        (ctx_index % parts_per_head) * column_width,
+        column_width,
+        1,
+    ).astype(jnp.float32)
+    peak = jnp.maximum(jnp.max(span_max, axis=0), own_score)
+    factor = jnp.exp(span_max - peak)
+    new_factor = jnp.exp(own_score - peak)
+    total_sum = jnp.sum(span_sum * factor, axis=0) + new_factor
+    merged = jnp.sum(span_out * factor[..., None], axis=0) + new_factor[:, None] * own_value
+    own_columns = (merged / total_sum[:, None]).astype(jnp.bfloat16)
     partial_out = jnp.dot(own_columns, w_out[0], preferred_element_type=jnp.float32)
     width_dev = hidden.shape[1]
-    summed_all = lax.psum(partial_out, ("tp", "ctx"))
-    branch_out = lax.dynamic_slice_in_dim(
-        summed_all, lax.axis_index("ctx") * width_dev, width_dev, 1
+    pieces = (
+        partial_out.astype(jnp.bfloat16)
+        .reshape(request_count, ctx_count, width_dev)
+        .transpose(1, 0, 2)
     )
+    tp_count = lax.axis_size("tp")
+    pieces = jnp.broadcast_to(pieces[None], (tp_count,) + pieces.shape).reshape(
+        tp_count * ctx_count, request_count, width_dev
+    )
+    pieces = lax.all_to_all(pieces, ("tp", "ctx"), 0, 0, tiled=True)
+    branch_out = pieces.astype(jnp.float32).sum(axis=0)
     section_rows = (hidden_f + branch_out).astype(jnp.bfloat16)
     arrived = from_behind(section_rows, "section", 1)
     selector = (routing[0][:, None] == jnp.arange(request_count, dtype=jnp.int32)[None, :]).astype(

time: 264 us -> 62.1 us (0.24)
  waiting for transfers between devices: 184 us -> 12.4 us
  blocking collectives: 52.2 us -> 20.8 us
  starting transfers between devices: 3.27 us -> 17.5 us
  between operations: 14.2 us -> 0.81 us
    psum x1 -> x0, waiting for transfers between devices: 182 us -> none  [per_device(): summed_all = lax.psum(partial_out, ('tp', 'ctx'))]
    psum x2 -> x0, blocking collectives: 39.7 us -> none  [the longest x1 20.7 us: per_device(): lax.psum((block_sum * factor, block_out * factor[..., None]), 'ctx')]
    all_to_all x0 -> x1, blocking collectives: none -> 20.8 us  [per_device(): pieces = lax.all_to_all(pieces, ('tp', 'ctx'), 0, 0, tiled=True)]
    all_to_all x0 -> x2, starting transfers between devices: none -> 14.2 us  [the longest x1 10.1 us: spread(): return lax.all_to_all(copies, axis, 0, 0, tiled=True)]
    pmax x1 -> x0, blocking collectives: 12.5 us -> none  [per_device(): top_score = lax.pmax(block_max, 'ctx')]
    all_to_all x0 -> x2, waiting for transfers between devices: none -> 9.57 us  [the longest x1 4.9 us: spread(): return lax.all_to_all(copies, axis, 0, 0, tiled=True)]
  transfers between devices with their start and end apart: 2 -> 3, of which waited for: 2 -> 3; matrix products, arithmetic and copies ran while one was open for 0% -> 0% of each run, Pallas kernels for 0% -> 0%
where the time goes in v1:
time: 62.1 us; the launch traced here: 61.7 us
  blocking collectives  20.8 us (33%)
  starting transfers between devices  17.5 us (28%)
  waiting for transfers between devices  12.4 us (20%)
  matrix products  4.5 us (7%)
  other arithmetic  3.21 us (5%)
  local copies, waits for them, and re-layouts  2.43 us (4%)
  between operations  0.81 us (1%)
    all_to_all x1, blocking collectives, per_device(): pieces = lax.all_to_all(pieces, ('tp', 'ctx'), 0, 0, tiled=True)  20.8 us
    all_to_all x1, starting transfers between devices, spread(): return lax.all_to_all(copies, axis, 0, 0, tiled=True)  10.1 us
    all_to_all x1, waiting for transfers between devices, spread(): return lax.all_to_all(copies, axis, 0, 0, tiled=True)  4.9 us
    all_to_all x1, waiting for transfers between devices, per_device(): packed = lax.all_to_all(packed, 'ctx', 0, 0, tiled=True)  4.67 us
    all_to_all x1, starting transfers between devices, per_device(): packed = lax.all_to_all(packed, 'ctx', 0, 0, tiled=True)  4.08 us
    ppermute x1, starting transfers between devices, from_behind(): return lax.ppermute(value, axis, pairs)  3.32 us
    ppermute x1, waiting for transfers between devices, from_behind(): return lax.ppermute(value, axis, pairs)  2.87 us
  transfers between devices with their start and end apart: 3, of which 3 were waited for; matrix products, arithmetic and copies ran while one was open for 0% of the time, Pallas kernels for 0%

profile of v1, /device:TPU:1, one launch (start us, length us, event | category | flops | bytes accessed | tf_op | source)
XLA Modules:
  0.0 61.7 jit_solution(1747943749292228408)
XLA Ops:
  0.7 0.9 %fusion.17 = f32[4]{0:T(128)S(1)} fusion(bf16[4,512]{1,0:T(4,128)(2,1)} %param.11), kind=kLoop, calls=%fused_computation.30 | loop fusion | flops 6140 | bytes 4112 | tf_op jit(solution)/shard_map/reduce_sum | solution.py:59
  1.6 0.1 copy.73
  1.7 1.1 %fusion.6 = f32[4,128]{1,0:T(4,128)S(1)} fusion(bf16[1,512,128]{2,1,0:T(8,128)(2,1)} %param.14, bf16[4,512]{1,0:T(4,128)(2,1)} %param.11, f32[512]{0:T(512)} %bitcast.80), kind=kOutput, calls=%fused_computation.10 | convolution fusion | flops 530432 | bytes 139264 | tf_op jit(solution)/shard_map/dot_general | solution.py:61
  2.8 0.1 fusion.4
  2.9 1.2 %fusion.2 = f32[4,512]{1,0:T(4,128)S(1)} fusion(bf16[1,512,512]{2,1,0:T(8,128)(2,1)} %param.13, bf16[4,512]{1,0:T(4,128)(2,1)S(1)} %copy-done.4, f32[512]{0:T(512)S(1)} %bitcast.82), kind=kOutput, calls=%fused_computation.5 | convolution fusion | flops 2103296 | bytes 538624 | tf_op jit(solution)/shard_map/dot_general | solution.py:60
  4.2 0.7 %broadcast_in_dim.36 = f32[8,4,769]{2,1,0:T(4,128)} broadcast(f32[4,769]{1,0:T(4,128)S(1)} %pad_maximum_fusion.1), dimensions={1,2} | broadcast | bytes 110736 | tf_op jit(solution)/shard_map/broadcast_in_dim | solution.py:21
  4.8 10.1 %all-to-all-start = ((f32[8,4,769]{2,1,0:T(4,128)}), f32[8,4,769]{2,1,0:T(4,128)S(1)}, u32[]{:S(2)}, u32[]{:S(2)}) async-start(f32[8,4,769]{2,1,0:T(4,128)} %broadcast_in_dim.36), calls=%async_computation | async-start | bytes 229376 | tf_op jit(solution)/shard_map/all_to_all | solution.py:22
  15.0 0.1 multiply_cosine_fusion.1
  15.2 4.9 %all-to-all-done = f32[8,4,769]{2,1,0:T(4,128)S(1)} async-done(((f32[8,4,769]{2,1,0:T(4,128)}), f32[8,4,769]{2,1,0:T(4,128)S(1)}, u32[]{:S(2)}, u32[]{:S(2)}) %all-to-all-start) | async-done | bytes 98464 | tf_op jit(solution)/shard_map/all_to_all | solution.py:22
  20.2 0.1 fusion.31
  20.4 0.1 fusion.44
  20.7 0.2 fusion.36
  20.9 0.1 copy.88
  21.0 0.5 fusion.54
  21.5 0.1 copy.76
  21.6 0.2 fusion.8
  21.8 0.3 fusion.10
  22.3 0.1 copy.80
  22.5 0.1 copy.81
  22.6 0.7 %pad_maximum_fusion = f32[8,4,66]{2,1,0:T(4,128)} fusion(f32[8,4,1]{2,1,0:T(4,128)S(1)} %copy.81, f32[8,4,1]{2,1,0:T(4,128)S(1)} %copy.80, f32[8,4,64]{2,1,0:T(4,128)S(1)} %bitcast.79), kind=kLoop, calls=%fused_computation.22 | loop fusion | flops 4224 | bytes 16896 | tf_op jit(solution)/shard_map/concatenate | solution.py:116
  23.3 4.1 %all-to-all-start.1 = ((f32[8,4,66]{2,1,0:T(4,128)}), f32[8,4,66]{2,1,0:T(4,128)S(1)}, u32[]{:S(2)}, u32[]{:S(2)}) async-start(f32[8,4,66]{2,1,0:T(4,128)} %pad_maximum_fusion), calls=%async_computation.1 | async-start | bytes 32768 | tf_op jit(solution)/shard_map/all_to_all | solution.py:117
  27.4 4.7 %all-to-all-done.1 = f32[8,4,66]{2,1,0:T(4,128)S(1)} async-done(((f32[8,4,66]{2,1,0:T(4,128)}), f32[8,4,66]{2,1,0:T(4,128)S(1)}, u32[]{:S(2)}, u32[]{:S(2)}) %all-to-all-start.1) | async-done | bytes 8480 | tf_op jit(solution)/shard_map/all_to_all | solution.py:117
  32.0 0.2 fusion.53
  32.2 0.1 copy.84
  32.3 0.1 copy.96
  32.5 0.2 fusion.34
  32.9 0.2 convolution_convert_fusion
  33.3 20.8 %all_to_all.15 = bf16[64,4,512]{2,1,0:T(4,128)(2,1)S(1)} all-to-all(bf16[64,4,512]{2,1,0:T(4,128)(2,1)S(1)} %bitcast.76), channel_id=1, replica_groups=mesh['section'=8,'tp'=8,'ctx'=8] {'tp','ctx'}, dimensions={0} | all-to-all | bytes 524288 | tf_op jit(solution)/shard_map/all_to_all | solution.py:145
  54.1 0.6 copy-done.5
  54.7 3.3 %collective-permute-start = (bf16[4,512]{1,0:T(4,128)(2,1)S(1)}, bf16[4,512]{1,0:T(4,128)(2,1)S(1)}, u32[]{:S(2)}, u32[]{:S(2)}) collective-permute-start(bf16[4,512]{1,0:T(4,128)(2,1)S(1)} %fusion.18), channel_id=1, source_target_pairs={{0,64},{64,128},{128,192},{192,256},{256,320},{320,384},{384,448},... | collective-permute-start | bytes 12296 | tf_op jit(solution)/shard_map/ppermute | solution.py:17
  58.1 2.9 %collective-permute-done = bf16[4,512]{1,0:T(4,128)(2,1)S(1)} collective-permute-done((bf16[4,512]{1,0:T(4,128)(2,1)S(1)}, bf16[4,512]{1,0:T(4,128)(2,1)S(1)}, u32[]{:S(2)}, u32[]{:S(2)}) %collective-permute-start) | collective-permute-done | bytes 4128 | tf_op jit(solution)/shard_map/ppermute | solution.py:17
  60.9 0.8 %convolution_convert_fusion.1 = bf16[4,512]{1,0:T(4,128)(2,1)} fusion(bf16[4,512]{1,0:T(4,128)(2,1)S(1)} %collective-permute-done, s32[4]{0:T(128)S(1)} %bitcast.89), kind=kOutput, calls=%fused_computation.3 | convolution fusion | flops 18448 | bytes 8208 | tf_op jit(solution)/shard_map/dot_general | solution.py:152
  (47 shorter events, 1.1 us)
Async XLA Ops:
  0.6 20.4 %copy-start = (bf16[4,1024,128]{2,1,0:T(8,128)(2,1)S(1)}, bf16[4,1024,128]{2,1,0:T(8,128)(2,1)}, u32[]{:S(2)}) copy-start(bf16[4,1024,128]{2,1,0:T(8,128)(2,1)} %param.17) | copy-start | bytes 3145732
  0.6 2.1 %copy-start.3 = (bf16[1,512,128]{2,1,0:T(8,128)(2,1)S(1)}, bf16[1,512,128]{2,1,0:T(8,128)(2,1)}, u32[]{:S(2)}) copy-start(bf16[1,512,128]{2,1,0:T(8,128)(2,1)} %param.15) | copy-start | bytes 393220
  1.7 1.1 %copy-start.4 = (bf16[4,512]{1,0:T(4,128)(2,1)S(1)}, bf16[4,512]{1,0:T(4,128)(2,1)}, u32[]{:S(2)}) copy-start(bf16[4,512]{1,0:T(4,128)(2,1)} %param.11) | copy-start | bytes 12292
  1.7 1.1 %copy-start.6 = (f32[1,512]{1,0:T(1,128)S(1)}, f32[1,512]{1,0:T(1,128)}, u32[]{:S(2)}) copy-start(f32[1,512]{1,0:T(1,128)} %param.12) | copy-start | bytes 6148
  2.9 12.1 %copy-start.8 = (s32[4]{0:T(128)S(1)}, s32[4]{0:T(128)}, u32[]{:S(2)}) copy-start(s32[4]{0:T(128)} %param.19) | copy-start | bytes 52
  2.9 12.1 %copy-start.7 = (s32[4,1,2]{0,2,1:T(2,128)S(1)}, s32[4,1,2]{0,2,1:T(2,128)}, u32[]{:S(2)}) copy-start(s32[4,1,2]{0,2,1:T(2,128)} %param.20) | copy-start | bytes 100
  4.2 17.6 %copy-start.1 = (bf16[4,1024,128]{2,1,0:T(8,128)(2,1)S(1)}, bf16[4,1024,128]{2,1,0:T(8,128)(2,1)}, u32[]{:S(2)}) copy-start(bf16[4,1024,128]{2,1,0:T(8,128)(2,1)} %param.18) | copy-start | bytes 3145732
  4.8 15.3 %all-to-all-start = ((f32[8,4,769]{2,1,0:T(4,128)}), f32[8,4,769]{2,1,0:T(4,128)S(1)}, u32[]{:S(2)}, u32[]{:S(2)}) async-start(f32[8,4,769]{2,1,0:T(4,128)} %broadcast_in_dim.36), calls=%async_computation | async-start | bytes 229376 | tf_op jit(solution)/shard_map/all_to_all | solution.py:22
  21.8 11.1 %copy-start.2 = (bf16[1,64,4096]{2,1,0:T(8,128)(2,1)S(1)}, bf16[1,64,4096]{2,1,0:T(8,128)(2,1)}, u32[]{:S(2)}) copy-start(bf16[1,64,4096]{2,1,0:T(8,128)(2,1)} %param.16) | copy-start | bytes 1572868
  23.3 8.8 %all-to-all-start.1 = ((f32[8,4,66]{2,1,0:T(4,128)}), f32[8,4,66]{2,1,0:T(4,128)S(1)}, u32[]{:S(2)}, u32[]{:S(2)}) async-start(f32[8,4,66]{2,1,0:T(4,128)} %pad_maximum_fusion), calls=%async_computation.1 | async-start | bytes 32768 | tf_op jit(solution)/shard_map/all_to_all | solution.py:117
  54.1 0.6 copy-start.5
  54.7 6.2 %copy-start.9 = (s32[1,4]{1,0:T(1,128)S(1)}, s32[1,4]{1,0:T(1,128)}, u32[]{:S(2)}) copy-start(s32[1,4]{1,0:T(1,128)} %param.21) | copy-start | bytes 52
  54.7 6.2 %collective-permute-start = (bf16[4,512]{1,0:T(4,128)(2,1)S(1)}, bf16[4,512]{1,0:T(4,128)(2,1)S(1)}, u32[]{:S(2)}, u32[]{:S(2)}) collective-permute-start(bf16[4,512]{1,0:T(4,128)(2,1)S(1)} %fusion.18), channel_id=1, source_target_pairs={{0,64},{64,128},{128,192},{192,256},{256,320},{320,384},{384,448},... | collective-permute-start | bytes 12296 | tf_op jit(solution)/shard_map/ppermute | solution.py:17

commit v2 on v0

v2 whole, which is shorter than its diff:
```python
import functools

import jax
import jax.numpy as jnp
import numpy as np
from jax import lax
from jax.experimental import pallas as pl
from jax.experimental.pallas import tpu as pltpu
from jax.sharding import PartitionSpec as P

HEAD_SIZE = 128
EPSILON = 1e-05
NEGATIVE = -1e30
ROPE_BASE = 500000.0
CTX = ("x", "core")
SCALE = HEAD_SIZE ** (-0.5)
PROJECT_INPUTS = (
    "lengths",
    "plan",
    "frequency",
    "hidden",
    "gain",
    "w_query",
    "w_key",
    "w_value",
    "keys",
    "values",
    "w_out",
)
PROJECT_OUTPUTS = ("parts", "table", "hidden", "keys", "values", "w_out")
F32 = jnp.float32
BF16 = jnp.bfloat16


def whole(memory_space=pltpu.VMEM):
    return pl.BlockSpec(memory_space=memory_space)


def in_vmem(value):
    return pltpu.with_memory_space_constraint(value, pltpu.VMEM)


def project(*refs):
    count = len(PROJECT_INPUTS)
    sources = dict(zip(PROJECT_INPUTS, refs))
    outputs = dict(zip(PROJECT_OUTPUTS, refs[count:]))
    scratch = refs[count + len(PROJECT_OUTPUTS) :]
    held = dict(zip(PROJECT_INPUTS, scratch))
    held.update(keys=outputs["keys"], values=outputs["values"], w_out=outputs["w_out"])
    semaphores = scratch[-1]
    copies = {
        name: pltpu.make_async_copy(sources[name], held[name], semaphores.at[at])
        for at, name in enumerate(PROJECT_INPUTS)
    }
    for name in PROJECT_INPUTS:
        copies[name].start()

    out_ref, table_ref = outputs["parts"], outputs["table"]
    for name in ("lengths", "plan", "frequency"):
        copies[name].wait()
    lengths_ref, plan_ref = held["lengths"], held["plan"]
    requests = lengths_ref.shape[0]
    row = lax.broadcasted_iota(jnp.int32, (requests, HEAD_SIZE), 0)
    lane = lax.broadcasted_iota(jnp.int32, (requests, HEAD_SIZE), 1)
    length = jnp.zeros((requests, HEAD_SIZE), jnp.int32)
    live = jnp.zeros((requests, HEAD_SIZE), jnp.int32)
    for request in range(requests):
        length = jnp.where(row == request, lengths_ref[request], length)
        live = jnp.where(row == request, plan_ref[0, 1, request] - plan_ref[0, 0, request], live)
    angles = length.astype(F32) * held["frequency"][...]
    sine = jnp.sin(angles)
    table_ref[:, :HEAD_SIZE] = jnp.cos(angles)
    table_ref[:, HEAD_SIZE : 2 * HEAD_SIZE] = jnp.where(lane < HEAD_SIZE // 2, -sine, sine)
    table_ref[:, 2 * HEAD_SIZE :] = live.astype(F32)

    for name in ("hidden", "gain"):
        copies[name].wait()
    hidden = held["hidden"][...].astype(F32)
    outputs["hidden"][...] = hidden
    scaled = (hidden * held["gain"][...]).astype(BF16)
    squares = jnp.sum(hidden * hidden, axis=1, keepdims=True)
    squares = jnp.broadcast_to(squares, (requests, HEAD_SIZE))
    at = 0
    for name in ("w_query", "w_key", "w_value"):
        copies[name].wait()
        part = jnp.dot(scaled, held[name][0], preferred_element_type=F32)
        width = part.shape[1]
        for peer in range(out_ref.shape[0]):
            out_ref[peer, :, at : at + width] = part
        at += width
    for peer in range(out_ref.shape[0]):
        out_ref[peer, :, at:] = squares
    for name in ("keys", "values", "w_out"):
        copies[name].wait()


def attend(model_width, parts_ref, table_ref, keys_ref, values_ref, out_ref):
    total = parts_ref[0]
    for peer in range(1, parts_ref.shape[0]):
        total = total + parts_ref[peer]
    requests, heads = keys_ref.shape[0], 4
    rows = heads * requests
    slots = keys_ref.shape[1]
    squares = total[:, 6 * HEAD_SIZE : 6 * HEAD_SIZE + 1]
    inverse = lax.rsqrt(squares / model_width + EPSILON)
    cosine = table_ref[:, :HEAD_SIZE]
    sine = table_ref[:, HEAD_SIZE : 2 * HEAD_SIZE]

    def rotated(at):
        part = total[:, at * HEAD_SIZE : (at + 1) * HEAD_SIZE] * inverse
        return part * cosine + pltpu.roll(part, HEAD_SIZE // 2, 1) * sine

    query = jnp.concatenate([rotated(head) for head in range(heads)], axis=0).astype(BF16)
    new_key = rotated(heads).astype(BF16).astype(F32)
    new_value = total[:, 5 * HEAD_SIZE : 6 * HEAD_SIZE] * inverse
    new_value = new_value.astype(BF16).astype(F32)
    request_of_row = lax.broadcasted_iota(jnp.int32, (rows, 1), 0) % requests

    scores = jnp.zeros((rows, slots), F32)
    for request in range(requests):
        own = lax.dot_general(
            query, keys_ref[request], (((1,), (1,)), ((), ())), preferred_element_type=F32
        )
        scores = jnp.where(request_of_row == request, own, scores)
    counts = jnp.concatenate([table_ref[:, 2 * HEAD_SIZE : 2 * HEAD_SIZE + 1]] * heads, axis=0)
    slot = lax.broadcasted_iota(jnp.int32, (rows, slots), 1)
    live = slot < counts.astype(jnp.int32)
    scores = jnp.where(live, scores * SCALE, NEGATIVE)
    block_max = jnp.max(scores, axis=1, keepdims=True)
    weights = jnp.where(live, jnp.exp(scores - block_max), 0.0)
    block_sum = jnp.sum(weights, axis=1, keepdims=True)
    weights = weights.astype(BF16)
    block_out = jnp.zeros((rows, HEAD_SIZE), F32)
    for request in range(requests):
        own = jnp.dot(weights, values_ref[request], preferred_element_type=F32)
        block_out = jnp.where(request_of_row == request, own, block_out)

    new_key = jnp.concatenate([new_key] * heads, axis=0)
    new_value = jnp.concatenate([new_value] * heads, axis=0)
    new_score = jnp.sum(query.astype(F32) * new_key, axis=1, keepdims=True) * SCALE
    takes_new = (lax.axis_index("x") == 0) & (lax.axis_index("core") == 0)
    peak = jnp.where(takes_new, jnp.maximum(block_max, new_score), block_max)
    factor = jnp.exp(block_max - peak)
    new_factor = jnp.where(takes_new, jnp.exp(new_score - peak), 0.0)
    block_sum = block_sum * factor + new_factor
    block_out = block_out * factor + new_factor * new_value

    lane = lax.broadcasted_iota(jnp.int32, (rows, HEAD_SIZE), 1)
    half = HEAD_SIZE // 2
    statistics = jnp.where(lane == half, peak, block_sum)
    lower = jnp.where(lane < half, block_out, statistics)
    upper = jnp.where(lane < half, pltpu.roll(block_out, half, 1), statistics)
    for head in range(heads):
        own = slice(head * requests, (head + 1) * requests)
        out_ref[2 * head] = lower[own]
        out_ref[2 * head + 1] = upper[own]


def merge_and_project(parts_ref, w_ref, out_ref):
    half = HEAD_SIZE // 2
    parts = parts_ref[...]
    span_max = parts[:, :, half : half + 1]
    peak = jnp.max(span_max, axis=0, keepdims=True)
    merged = jnp.sum(parts * jnp.exp(span_max - peak), axis=0)
    attended = (merged / merged[:, half + 1 : half + 2])[:, :half].astype(BF16)
    result = jnp.dot(attended, w_ref[0], preferred_element_type=F32).astype(BF16)
    peers, width = out_ref.shape[0], out_ref.shape[2]
    columns = result.shape[1] // width
    for peer in range(peers):
        at = peer % columns * width
        out_ref[peer] = result[:, at : at + width]


def from_behind(value, axis, steps):
    count = lax.axis_size(axis)
    return lax.ppermute(value, axis, [(source, (source + steps) % count) for source in range(count)])


def frequencies():
    half_dim = HEAD_SIZE // 2
    frequency = ROPE_BASE ** (-2.0 * np.arange(half_dim) / HEAD_SIZE)
    return np.concatenate([frequency, frequency])[None, :].astype(np.float32)


def per_device(
    hidden,
    gain,
    w_query,
    key_weight,
    value_weight,
    w_out,
    key_cache_slots,
    value_cache_slots,
    lengths,
    plan,
    routing,
):
    requests, width = hidden.shape
    ctx_count = lax.axis_size(CTX)
    packed_width = w_query.shape[2] + 2 * key_weight.shape[2] + HEAD_SIZE
    sources = (
        lengths,
        jnp.transpose(plan, (1, 2, 0)),
        jnp.asarray(frequencies()),
        hidden,
        gain,
        w_query,
        key_weight,
        value_weight,
        key_cache_slots,
        value_cache_slots,
        w_out,
    )
    moved = sources[-3:]
    parts, table, hidden_f, keys, values, w_out = pl.pallas_call(
        project,
        out_shape=(
            pltpu.VMEM((ctx_count, requests, packed_width), F32),
            pltpu.VMEM((requests, 3 * HEAD_SIZE), F32),
            pltpu.VMEM((requests, width), F32),
        )
        + tuple(pltpu.VMEM(source.shape, source.dtype) for source in moved),
        in_specs=[whole(pltpu.HBM)] * len(sources),
        out_specs=(whole(),) * 6,
        scratch_shapes=[
            (pltpu.SMEM if source.dtype == jnp.int32 else pltpu.VMEM)(source.shape, source.dtype)
            for source in sources[:-3]
        ]
        + [pltpu.SemaphoreType.DMA((len(sources),))],
        name="project",
        compiler_params=pltpu.CompilerParams(vmem_limit_bytes=16 * 2**20),
    )(*[pltpu.with_memory_space_constraint(source, pltpu.HBM) for source in sources])
    parts = lax.all_to_all(parts, CTX, 0, 0, tiled=True)
    spans = pl.pallas_call(
        functools.partial(attend, width * ctx_count),
        out_shape=pltpu.VMEM((ctx_count, requests, HEAD_SIZE), F32),
        in_specs=[whole()] * 4,
        out_specs=whole(),
        name="attend",
        compiler_params=pltpu.CompilerParams(vmem_limit_bytes=16 * 2**20),
    )(parts, table, in_vmem(keys), in_vmem(values))
    spans = lax.all_to_all(spans, CTX, 0, 0, tiled=True)
    pieces = pl.pallas_call(
        merge_and_project,
        out_shape=pltpu.VMEM((lax.axis_size("tp") * ctx_count, requests, width), BF16),
        in_specs=[whole()] * 2,
        out_specs=whole(),
        name="merge_and_project",
    )(spans, in_vmem(w_out))
    pieces = lax.all_to_all(pieces, ("tp",) + CTX, 0, 0, tiled=True)
    section_rows = (hidden_f + pieces.astype(F32).sum(axis=0)).astype(BF16)
    section_rows, pieces = lax.optimization_barrier((section_rows, pieces))
    arrived = from_behind(section_rows, "section", 1)
    branch_out = pieces.astype(F32).sum(axis=0)
    selector = (routing[0][:, None] == jnp.arange(requests, dtype=jnp.int32)[None, :]).astype(BF16)
    handed = jnp.dot(selector, arrived, preferred_element_type=F32).astype(BF16)
    return (handed, branch_out)


def solution(mesh):
    sizes = mesh.shape
    devices = mesh.devices.reshape(sizes["section"], sizes["tp"], sizes["ctx"] // 2, 2)
    mesh = jax.sharding.Mesh(devices, ("section", "tp", "x", "core"))
    return jax.shard_map(
        per_device,
        mesh=mesh,
        in_specs=(
            P("section", CTX),
            P("section", CTX),
            P("section", CTX, "tp"),
            P("section", CTX, "tp"),
            P("section", CTX, "tp"),
            P("section", ("tp",) + CTX, None),
            P("section", CTX, "tp"),
            P("section", CTX, "tp"),
            P("section"),
            P("section", CTX, None),
            P("section", None),
        ),
        out_specs=(P("section", CTX), P("section", CTX)),
        check_vma=False,
    )
```

time: 264 us -> 56.4 us (0.21)
  waiting for transfers between devices: 184 us -> 2.13 us
  between operations: 14.2 us -> 0.66 us
  blocking collectives: 52.2 us -> 44.4 us
  matrix products: 5.15 us -> 0.78 us
  Pallas kernels: 0 us -> 4.03 us
  other arithmetic: 4.5 us -> 0.89 us
    psum x1 -> x0, waiting for transfers between devices: 182 us -> none  [per_device(): summed_all = lax.psum(partial_out, ('tp', 'ctx'))]
    all_to_all x0 -> x3, blocking collectives: none -> 44.4 us  [the longest x1 21.5 us: per_device(): pieces = lax.all_to_all(pieces, ('tp',) + CTX, 0, 0, tiled=True)]
    psum x2 -> x0, blocking collectives: 39.7 us -> none  [the longest x1 20.7 us: per_device(): lax.psum((block_sum * factor, block_out * factor[..., None]), 'ctx')]
    pmax x1 -> x0, blocking collectives: 12.5 us -> none  [per_device(): top_score = lax.pmax(block_max, 'ctx')]
    dot_general x8 -> x1, matrix products: 5.15 us -> 0.78 us  [per_device(): handed = jnp.dot(selector, arrived, preferred_element_type=F32).astype(BF16)]
    pallas_call x0 -> x3, Pallas kernels: none -> 4.03 us  [the longest x1 2.06 us: per_device(): pl.pallas_call(project, out_shape=(pltpu.VMEM((ctx_count, requests, packe...]
  transfers between devices with their start and end apart: 2 -> 1, of which waited for: 2 -> 1; matrix products, arithmetic and copies ran while one was open for 0% -> 1% of each run, Pallas kernels for 0% -> 0%
where the time goes in v2:
time: 56.4 us; the launch traced here: 56.1 us
  blocking collectives  44.4 us (79%)
  Pallas kernels  4.03 us (7%)
  starting transfers between devices  3.2 us (6%)
  waiting for transfers between devices  2.13 us (4%)
  other arithmetic  0.89 us (2%)
  matrix products  0.78 us (1%)
  between operations  0.66 us (1%)
    all_to_all x1, blocking collectives, per_device(): pieces = lax.all_to_all(pieces, ('tp',) + CTX, 0, 0, tiled=True)  21.5 us
    all_to_all x1, blocking collectives, per_device(): parts = lax.all_to_all(parts, CTX, 0, 0, tiled=True)  14.4 us
    all_to_all x1, blocking collectives, per_device(): spans = lax.all_to_all(spans, CTX, 0, 0, tiled=True)  8.54 us
    ppermute x1, starting transfers between devices, from_behind(): lax.ppermute(value, axis, [(source, (source + steps) % count) for source...  3.2 us
    ppermute x1, waiting for transfers between devices, from_behind(): lax.ppermute(value, axis, [(source, (source + steps) % count) for source...  2.13 us
    pallas_call x1, Pallas kernels, per_device(): pl.pallas_call(project, out_shape=(pltpu.VMEM((ctx_count, requests, packe...  2.06 us
  transfers between devices with their start and end apart: 1, of which 1 were waited for; matrix products, arithmetic and copies ran while one was open for 1% of the time, Pallas kernels for 0%

profile of v2, /device:TPU:1, one launch (start us, length us, event | category | flops | bytes accessed | tf_op | source)
XLA Modules:
  0.0 56.1 jit_solution(7870386652737260267)
XLA Ops:
  0.6 2.1 %project.1 = (f32[8,4,896]{2,1,0:T(4,128)S(1)}, f32[4,384]{1,0:T(4,128)S(1)}, f32[4,512]{1,0:T(4,128)S(1)}, bf16[4,1024,128]{2,1,0:T(8,128)(2,1)S(1)}, bf16[4,10...) custom-call(s32[4]{0:T(128)} %refs_0_.1, s32[1,2,4]{2,1,0:T(2,128)} %bitcast.3, ...), custom_call_target="tpu_custom_call" | custom-call | tf_op jit(solution)/shard_map/project/pallas_call | solution.py:215
  2.7 14.4 %all_to_all.15.parts_ref = f32[8,4,896]{2,1,0:T(4,128)S(1)} all-to-all(f32[8,4,896]{2,1,0:T(4,128)S(1)} %get-tuple-element.11), channel_id=1, replica_groups=mesh['section'=8,'tp'=8,'x'=4,'core'=2] {'x','core'}, dimensions={0} | all-to-all | bytes 229376 | tf_op jit(solution)/shard_map/all_to_all | solution.py:233
  17.1 0.9 %attend.1 = f32[8,4,128]{2,1,0:T(4,128)S(1)} custom-call(f32[8,4,896]{2,1,0:T(4,128)S(1)} %all_to_all.15.parts_ref, f32[4,384]{1,0:T(4,128)S(1)} %get-tuple-element.12.table_ref, bf16[4,1024,128]{2,1,0:T(8,128)(2,1)S(1)} %get-tuple-element.13.keys_ref, bf16[4,1024,128]{2,1,0:T(8,128)(2,1)S(1)} %get-tuple-element.14.values_ref), custom_call_target="tpu_custom_call" | custom-call | tf_op jit(solution)/shard_map/attend/pallas_call | solution.py:234
  18.0 8.5 %all_to_all.16.parts_ref = f32[8,4,128]{2,1,0:T(4,128)} all-to-all(f32[8,4,128]{2,1,0:T(4,128)S(1)} %attend.1), channel_id=1, replica_groups=mesh['section'=8,'tp'=8,'x'=4,'core'=2] {'x','core'}, dimensions={0} | all-to-all | bytes 32768 | tf_op jit(solution)/shard_map/all_to_all | solution.py:242
  26.5 1.1 %merge_and_project.1 = bf16[64,4,512]{2,1,0:T(4,128)(2,1)S(1)} custom-call(f32[8,4,128]{2,1,0:T(4,128)} %all_to_all.16.parts_ref, bf16[1,64,4096]{2,1,0:T(8,128)(2,1)S(1)} %get-tuple-element.15.w_ref), custom_call_target="tpu_custom_call" | custom-call | tf_op jit(solution)/shard_map/merge_and_project/pallas_call | solution.py:243
  27.6 21.5 %all_to_all.17 = bf16[64,4,512]{2,1,0:T(4,128)(2,1)S(1)} all-to-all(bf16[64,4,512]{2,1,0:T(4,128)(2,1)S(1)} %merge_and_project.1), channel_id=1, replica_groups=mesh['section'=8,'tp'=8,'x'=4,'core'=2] {'tp','x','core'}, dimensions={0} | all-to-all | bytes 524288 | tf_op jit(solution)/shard_map/all_to_all | solution.py:250
  49.1 0.1 convert_reduce_fusion.1
  49.2 3.2 %collective-permute-start = (bf16[4,512]{1,0:T(4,128)(2,1)S(1)}, bf16[4,512]{1,0:T(4,128)(2,1)S(1)}, u32[]{:S(2)}, u32[]{:S(2)}) collective-permute-start(bf16[4,512]{1,0:T(4,128)(2,1)S(1)} %add_convert_fusion), channel_id=1, source_target_pairs={{0,64},{64,128},{128,192},{192,256},{256,320},{320,384},{384,448},... | collective-permute-start | bytes 12296 | tf_op jit(solution)/shard_map/ppermute | solution.py:176
  52.4 0.7 %convert_reduce_fusion = f32[4,512]{1,0:T(4,128)} fusion(bf16[64,4,512]{2,1,0:T(4,128)(2,1)S(1)} %all_to_all.17), kind=kLoop, calls=%fused_computation.1 | loop fusion | flops 260096 | bytes 270336 | tf_op jit(solution)/shard_map/reduce_sum | solution.py:254
  53.2 0.0 copy-start
  53.2 2.1 %collective-permute-done = bf16[4,512]{1,0:T(4,128)(2,1)S(1)} collective-permute-done((bf16[4,512]{1,0:T(4,128)(2,1)S(1)}, bf16[4,512]{1,0:T(4,128)(2,1)S(1)}, u32[]{:S(2)}, u32[]{:S(2)}) %collective-permute-start) | collective-permute-done | bytes 4128 | tf_op jit(solution)/shard_map/ppermute | solution.py:176
  55.3 0.0 copy-done
  55.3 0.8 %convolution_convert_fusion = bf16[4,512]{1,0:T(4,128)(2,1)} fusion(bf16[4,512]{1,0:T(4,128)(2,1)S(1)} %collective-permute-done, s32[4]{0:T(128)S(1)} %bitcast.4), kind=kOutput, calls=%fused_computation | convolution fusion | flops 18448 | bytes 8208 | tf_op jit(solution)/shard_map/dot_general | solution.py:256
  (1 shorter events, 0.0 us)
Async XLA Ops:
  49.2 6.1 %collective-permute-start = (bf16[4,512]{1,0:T(4,128)(2,1)S(1)}, bf16[4,512]{1,0:T(4,128)(2,1)S(1)}, u32[]{:S(2)}, u32[]{:S(2)}) collective-permute-start(bf16[4,512]{1,0:T(4,128)(2,1)S(1)} %add_convert_fusion), channel_id=1, source_target_pairs={{0,64},{64,128},{128,192},{192,256},{256,320},{320,384},{384,448},... | collective-permute-start | bytes 12296 | tf_op jit(solution)/shard_map/ppermute | solution.py:176
  53.2 2.1 %copy-start = (s32[1,4]{1,0:T(1,128)S(1)}, s32[1,4]{1,0:T(1,128)}, u32[]{:S(2)}) copy-start(s32[1,4]{1,0:T(1,128)} %param.22) | copy-start | bytes 52

commit v3 on v2

--- a/solution.py
+++ b/solution.py
@@ -12,7 +12,8 @@
 EPSILON = 1e-05
 NEGATIVE = -1e30
 ROPE_BASE = 500000.0
-CTX = ("x", "core")
+CTX = ("far", "near", "core")
+LAST = ("tp", "near", "core")
 SCALE = HEAD_SIZE ** (-0.5)
 PROJECT_INPUTS = (
     "lengths",
@@ -138,7 +139,7 @@
     new_key = jnp.concatenate([new_key] * heads, axis=0)
     new_value = jnp.concatenate([new_value] * heads, axis=0)
     new_score = jnp.sum(query.astype(F32) * new_key, axis=1, keepdims=True) * SCALE
-    takes_new = (lax.axis_index("x") == 0) & (lax.axis_index("core") == 0)
+    takes_new = lax.axis_index(CTX) == 0
     peak = jnp.where(takes_new, jnp.maximum(block_max, new_score), block_max)
     factor = jnp.exp(block_max - peak)
     new_factor = jnp.where(takes_new, jnp.exp(new_score - peak), 0.0)
@@ -151,20 +152,26 @@
     lower = jnp.where(lane < half, block_out, statistics)
     upper = jnp.where(lane < half, pltpu.roll(block_out, half, 1), statistics)
     for head in range(heads):
-        own = slice(head * requests, (head + 1) * requests)
-        out_ref[2 * head] = lower[own]
-        out_ref[2 * head + 1] = upper[own]
-
-
-def merge_and_project(parts_ref, w_ref, out_ref):
+        for place, source in enumerate((head, head ^ 2)):
+            rows_of = slice(source * requests, (source + 1) * requests)
+            to = slice(place * requests, (place + 1) * requests)
+            out_ref[2 * head, to] = lower[rows_of]
+            out_ref[2 * head + 1, to] = upper[rows_of]
+
+
+def merge_and_project(parts_ref, kept_ref, swapped_ref, out_ref):
     half = HEAD_SIZE // 2
     parts = parts_ref[...]
     span_max = parts[:, :, half : half + 1]
     peak = jnp.max(span_max, axis=0, keepdims=True)
     merged = jnp.sum(parts * jnp.exp(span_max - peak), axis=0)
-    attended = (merged / merged[:, half + 1 : half + 2])[:, :half].astype(BF16)
-    result = jnp.dot(attended, w_ref[0], preferred_element_type=F32).astype(BF16)
-    peers, width = out_ref.shape[0], out_ref.shape[2]
+    attended = merged / merged[:, half + 1 : half + 2]
+    peers, requests, width = out_ref.shape
+    own = attended[:requests, :half].astype(BF16)
+    far = attended[requests:, :half].astype(BF16)
+    result = jnp.dot(own, kept_ref[...], preferred_element_type=F32)
+    result += jnp.dot(far, swapped_ref[...], preferred_element_type=F32)
+    result = result.astype(BF16)
     columns = result.shape[1] // width
     for peer in range(peers):
         at = peer % columns * width
@@ -230,24 +237,30 @@
         name="project",
         compiler_params=pltpu.CompilerParams(vmem_limit_bytes=16 * 2**20),
     )(*[pltpu.with_memory_space_constraint(source, pltpu.HBM) for source in sources])
+    parts, w_rows = lax.optimization_barrier((parts, w_out[0]))
+    half_columns = w_rows.shape[1] // 2
+    far = lax.axis_index("far")
+    w_kept = lax.dynamic_slice_in_dim(w_rows, far * half_columns, half_columns, 1)
+    w_sent = lax.dynamic_slice_in_dim(w_rows, (1 - far) * half_columns, half_columns, 1)
+    w_swapped = from_behind(w_sent, "far", 1)
     parts = lax.all_to_all(parts, CTX, 0, 0, tiled=True)
     spans = pl.pallas_call(
         functools.partial(attend, width * ctx_count),
-        out_shape=pltpu.VMEM((ctx_count, requests, HEAD_SIZE), F32),
+        out_shape=pltpu.VMEM((ctx_count, 2 * requests, HEAD_SIZE), F32),
         in_specs=[whole()] * 4,
         out_specs=whole(),
         name="attend",
         compiler_params=pltpu.CompilerParams(vmem_limit_bytes=16 * 2**20),
-    )(parts, table, in_vmem(keys), in_vmem(values))
+    )(in_vmem(parts), in_vmem(table), in_vmem(keys), in_vmem(values))
     spans = lax.all_to_all(spans, CTX, 0, 0, tiled=True)
     pieces = pl.pallas_call(
         merge_and_project,
-        out_shape=pltpu.VMEM((lax.axis_size("tp") * ctx_count, requests, width), BF16),
-        in_specs=[whole()] * 2,
+        out_shape=pltpu.VMEM((lax.axis_size(LAST), requests, width), BF16),
+        in_specs=[whole()] * 3,
         out_specs=whole(),
         name="merge_and_project",
-    )(spans, in_vmem(w_out))
-    pieces = lax.all_to_all(pieces, ("tp",) + CTX, 0, 0, tiled=True)
+    )(in_vmem(spans), in_vmem(w_kept), in_vmem(w_swapped))
+    pieces = lax.all_to_all(pieces, LAST, 0, 0, tiled=True)
     section_rows = (hidden_f + pieces.astype(F32).sum(axis=0)).astype(BF16)
     section_rows, pieces = lax.optimization_barrier((section_rows, pieces))
     arrived = from_behind(section_rows, "section", 1)
@@ -259,8 +272,8 @@
 
 def solution(mesh):
     sizes = mesh.shape
-    devices = mesh.devices.reshape(sizes["section"], sizes["tp"], sizes["ctx"] // 2, 2)
-    mesh = jax.sharding.Mesh(devices, ("section", "tp", "x", "core"))
+    devices = mesh.devices.reshape(sizes["section"], sizes["tp"], 2, 2, 2)
+    mesh = jax.sharding.Mesh(devices, ("section", "tp") + CTX)
     return jax.shard_map(
         per_device,
         mesh=mesh,

time: 56.4 us -> 54.5 us (0.966)
  blocking collectives: 44.4 us -> 37.8 us
  starting transfers between devices: 3.2 us -> 8.69 us
  Pallas kernels: 4.03 us -> 3.32 us
    ppermute x1 -> x2, starting transfers between devices: 3.2 us -> 8.69 us  [from_behind(): lax.ppermute(value, axis, [(source, (source + steps) % count) for source...]
    all_to_all x1, blocking collectives: 21.5 us -> 16.8 us  [per_device(): pieces = lax.all_to_all(pieces, LAST, 0, 0, tiled=True)]
    all_to_all x1, blocking collectives: 14.4 us -> 13 us  [per_device(): parts = lax.all_to_all(parts, CTX, 0, 0, tiled=True)]
    pallas_call x1, Pallas kernels: 1.06 us -> 0.35 us  [per_device(): pl.pallas_call(merge_and_project, out_shape=pltpu.VMEM((lax.axis_size(LAS...]
    all_to_all x1, blocking collectives: 8.54 us -> 7.92 us  [per_device(): spans = lax.all_to_all(spans, CTX, 0, 0, tiled=True)]
    ppermute x1 -> x2, waiting for transfers between devices: 2.13 us -> 2.2 us  [from_behind(): lax.ppermute(value, axis, [(source, (source + steps) % count) for source...]
  transfers between devices with their start and end apart: 1 -> 2, of which waited for: 1 -> 1; matrix products, arithmetic and copies ran while one was open for 1% -> 1% of each run, Pallas kernels for 0% -> 2%
where the time goes in v3:
time: 54.5 us; the launch traced here: 54.2 us
  blocking collectives  37.8 us (69%)
  starting transfers between devices  8.69 us (16%)
  Pallas kernels  3.32 us (6%)
  waiting for transfers between devices  2.2 us (4%)
  matrix products  0.78 us (1%)
  other arithmetic  0.75 us (1%)
  between operations  0.69 us (1%)
    all_to_all x1, blocking collectives, per_device(): pieces = lax.all_to_all(pieces, LAST, 0, 0, tiled=True)  16.8 us
    all_to_all x1, blocking collectives, per_device(): parts = lax.all_to_all(parts, CTX, 0, 0, tiled=True)  13 us
    ppermute x2, starting transfers between devices, from_behind(): lax.ppermute(value, axis, [(source, (source + steps) % count) for source...  8.69 us
    all_to_all x1, blocking collectives, per_device(): spans = lax.all_to_all(spans, CTX, 0, 0, tiled=True)  7.92 us
    ppermute x2, waiting for transfers between devices, from_behind(): lax.ppermute(value, axis, [(source, (source + steps) % count) for source...  2.2 us
    pallas_call x1, Pallas kernels, per_device(): pl.pallas_call(project, out_shape=(pltpu.VMEM((ctx_count, requests, packe...  2.06 us
  transfers between devices with their start and end apart: 2, of which 1 were waited for; matrix products, arithmetic and copies ran while one was open for 1% of the time, Pallas kernels for 2%

profile of v3, /device:TPU:1, one launch (start us, length us, event | category | flops | bytes accessed | tf_op | source)
XLA Modules:
  0.0 54.2 jit_solution(7566547059594272879)
XLA Ops:
  0.6 2.1 %project.1 = (f32[8,4,896]{2,1,0:T(4,128)S(1)}, f32[4,384]{1,0:T(4,128)S(1)}, f32[4,512]{1,0:T(4,128)S(1)}, bf16[4,1024,128]{2,1,0:T(8,128)(2,1)S(1)}, bf16[4,10...) custom-call(s32[4]{0:T(128)} %refs_0_.1, s32[1,2,4]{2,1,0:T(2,128)} %bitcast.5, ...), custom_call_target="tpu_custom_call" | custom-call | tf_op jit(solution)/shard_map/project/pallas_call | solution.py:222
  2.8 5.5 %collective-permute-start = (bf16[64,2048]{1,0:T(8,128)(2,1)S(1)}, bf16[64,2048]{1,0:T(8,128)(2,1)S(1)}, u32[]{:S(2)}, u32[]{:S(2)}) collective-permute-start(bf16[64,2048]{1,0:T(8,128)(2,1)S(1)} %get-tuple-element.22), channel_id=1, source_target_pairs={{0,4},{4,0},{1,5},{5,1},{2,6},{6,2},{3,7},{7,3},{8,12},{12,8},{9,1... | collective-permute-start | bytes 786440 | tf_op jit(solution)/shard_map/ppermute | solution.py:183
  8.3 13.0 %all_to_all.15.parts_ref = f32[8,4,896]{2,1,0:T(4,128)S(1)} all-to-all(f32[8,4,896]{2,1,0:T(4,128)S(1)} %get-tuple-element.15), channel_id=1, replica_groups=mesh['section'=8,'tp'=8,'far'=2,'near'=2,'core'=2] {'far','near','core'}, dimensions={0} | all-to-all | bytes 229376 | tf_op jit(solution)/shard_map/all_to_all | solution.py:246
  21.3 0.9 %attend.1 = f32[8,8,128]{2,1,0:T(8,128)S(1)} custom-call(f32[8,4,896]{2,1,0:T(4,128)S(1)} %all_to_all.15.parts_ref, f32[4,384]{1,0:T(4,128)S(1)} %get-tuple-element.16.table_ref, bf16[4,1024,128]{2,1,0:T(8,128)(2,1)S(1)} %get-tuple-element.17.keys_ref, bf16[4,1024,128]{2,1,0:T(8,128)(2,1)S(1)} %get-tuple-element.18.values_ref), custom_call_target="tpu_custom_call" | custom-call | tf_op jit(solution)/shard_map/attend/pallas_call | solution.py:247
  22.2 7.9 %all_to_all.16.parts_ref = f32[8,8,128]{2,1,0:T(8,128)S(1)} all-to-all(f32[8,8,128]{2,1,0:T(8,128)S(1)} %attend.1), channel_id=1, replica_groups=mesh['section'=8,'tp'=8,'far'=2,'near'=2,'core'=2] {'far','near','core'}, dimensions={0} | all-to-all | bytes 65536 | tf_op jit(solution)/shard_map/all_to_all | solution.py:255
  30.1 0.0 collective-permute-done.swapped_ref
  30.1 0.3 merge_and_project.1
  30.5 16.8 %all_to_all.17 = bf16[32,4,512]{2,1,0:T(4,128)(2,1)S(1)} all-to-all(bf16[32,4,512]{2,1,0:T(4,128)(2,1)S(1)} %merge_and_project.1), channel_id=1, replica_groups=mesh['section'=8,'tp'=8,'far'=2,'near'=2,'core'=2] {'tp','near','core'}, dimensions={0} | all-to-all | bytes 262144 | tf_op jit(solution)/shard_map/all_to_all | solution.py:263
  47.3 0.1 convert_reduce_fusion.1
  47.4 3.2 %collective-permute-start.1 = (bf16[4,512]{1,0:T(4,128)(2,1)S(1)}, bf16[4,512]{1,0:T(4,128)(2,1)S(1)}, u32[]{:S(2)}, u32[]{:S(2)}) collective-permute-start(bf16[4,512]{1,0:T(4,128)(2,1)S(1)} %add_convert_fusion), channel_id=1, source_target_pairs={{0,64},{64,128},{128,192},{192,256},{256,320},{320,384},{384,448},... | collective-permute-start | bytes 12296 | tf_op jit(solution)/shard_map/ppermute | solution.py:183
  50.6 0.7 %convert_reduce_fusion = f32[4,512]{1,0:T(4,128)} fusion(bf16[32,4,512]{2,1,0:T(4,128)(2,1)S(1)} %all_to_all.17), kind=kLoop, calls=%fused_computation.1 | loop fusion | flops 129024 | bytes 139264 | tf_op jit(solution)/shard_map/reduce_sum | solution.py:267
  51.2 0.0 copy-start
  51.2 2.2 %collective-permute-done.1 = bf16[4,512]{1,0:T(4,128)(2,1)S(1)} collective-permute-done((bf16[4,512]{1,0:T(4,128)(2,1)S(1)}, bf16[4,512]{1,0:T(4,128)(2,1)S(1)}, u32[]{:S(2)}, u32[]{:S(2)}) %collective-permute-start.1) | collective-permute-done | bytes 4128 | tf_op jit(solution)/shard_map/ppermute | solution.py:183
  53.4 0.0 copy-done
  53.5 0.8 %convolution_convert_fusion = bf16[4,512]{1,0:T(4,128)(2,1)} fusion(bf16[4,512]{1,0:T(4,128)(2,1)S(1)} %collective-permute-done.1, s32[4]{0:T(128)S(1)} %bitcast.6), kind=kOutput, calls=%fused_computation | convolution fusion | flops 18448 | bytes 8208 | tf_op jit(solution)/shard_map/dot_general | solution.py:269
  (2 shorter events, 0.1 us)
Async XLA Ops:
  2.8 27.4 %collective-permute-start = (bf16[64,2048]{1,0:T(8,128)(2,1)S(1)}, bf16[64,2048]{1,0:T(8,128)(2,1)S(1)}, u32[]{:S(2)}, u32[]{:S(2)}) collective-permute-start(bf16[64,2048]{1,0:T(8,128)(2,1)S(1)} %get-tuple-element.22), channel_id=1, source_target_pairs={{0,4},{4,0},{1,5},{5,1},{2,6},{6,2},{3,7},{7,3},{8,12},{12,8},{9,1... | collective-permute-start | bytes 786440 | tf_op jit(solution)/shard_map/ppermute | solution.py:183
  47.4 6.1 %collective-permute-start.1 = (bf16[4,512]{1,0:T(4,128)(2,1)S(1)}, bf16[4,512]{1,0:T(4,128)(2,1)S(1)}, u32[]{:S(2)}, u32[]{:S(2)}) collective-permute-start(bf16[4,512]{1,0:T(4,128)(2,1)S(1)} %add_convert_fusion), channel_id=1, source_target_pairs={{0,64},{64,128},{128,192},{192,256},{256,320},{320,384},{384,448},... | collective-permute-start | bytes 12296 | tf_op jit(solution)/shard_map/ppermute | solution.py:183
  51.2 2.2 %copy-start = (s32[1,4]{1,0:T(1,128)S(1)}, s32[1,4]{1,0:T(1,128)}, u32[]{:S(2)}) copy-start(s32[1,4]{1,0:T(1,128)} %param.22) | copy-start | bytes 52

commit v4 on v3

--- a/solution.py
+++ b/solution.py
@@ -15,20 +15,6 @@
 CTX = ("far", "near", "core")
 LAST = ("tp", "near", "core")
 SCALE = HEAD_SIZE ** (-0.5)
-PROJECT_INPUTS = (
-    "lengths",
-    "plan",
-    "frequency",
-    "hidden",
-    "gain",
-    "w_query",
-    "w_key",
-    "w_value",
-    "keys",
-    "values",
-    "w_out",
-)
-PROJECT_OUTPUTS = ("parts", "table", "hidden", "keys", "values", "w_out")
 F32 = jnp.float32
 BF16 = jnp.bfloat16
 
@@ -41,26 +27,26 @@
     return pltpu.with_memory_space_constraint(value, pltpu.VMEM)
 
 
-def project(*refs):
-    count = len(PROJECT_INPUTS)
-    sources = dict(zip(PROJECT_INPUTS, refs))
-    outputs = dict(zip(PROJECT_OUTPUTS, refs[count:]))
-    scratch = refs[count + len(PROJECT_OUTPUTS) :]
-    held = dict(zip(PROJECT_INPUTS, scratch))
-    held.update(keys=outputs["keys"], values=outputs["values"], w_out=outputs["w_out"])
-    semaphores = scratch[-1]
-    copies = {
-        name: pltpu.make_async_copy(sources[name], held[name], semaphores.at[at])
-        for at, name in enumerate(PROJECT_INPUTS)
-    }
-    for name in PROJECT_INPUTS:
-        copies[name].start()
-
-    out_ref, table_ref = outputs["parts"], outputs["table"]
-    for name in ("lengths", "plan", "frequency"):
-        copies[name].wait()
-    lengths_ref, plan_ref = held["lengths"], held["plan"]
-    requests = lengths_ref.shape[0]
+def project(
+    lengths_ref, plan_ref, frequency_ref, hidden_ref, gain_ref, query_ref, key_ref, value_ref,
+    out_ref, table_ref, hidden_out_ref,
+):
+    hidden = hidden_ref[...].astype(F32)
+    requests = hidden.shape[0]
+    hidden_out_ref[...] = hidden
+    scaled = (hidden * gain_ref[...]).astype(BF16)
+    squares = jnp.sum(hidden * hidden, axis=1, keepdims=True)
+    squares = jnp.broadcast_to(squares, (requests, HEAD_SIZE))
+    at = 0
+    for ref in (query_ref, key_ref, value_ref):
+        part = jnp.dot(scaled, ref[0], preferred_element_type=F32)
+        width = part.shape[1]
+        for peer in range(out_ref.shape[0]):
+            out_ref[peer, :, at : at + width] = part
+        at += width
+    for peer in range(out_ref.shape[0]):
+        out_ref[peer, :, at:] = squares
+
     row = lax.broadcasted_iota(jnp.int32, (requests, HEAD_SIZE), 0)
     lane = lax.broadcasted_iota(jnp.int32, (requests, HEAD_SIZE), 1)
     length = jnp.zeros((requests, HEAD_SIZE), jnp.int32)
@@ -68,31 +54,11 @@
     for request in range(requests):
         length = jnp.where(row == request, lengths_ref[request], length)
         live = jnp.where(row == request, plan_ref[0, 1, request] - plan_ref[0, 0, request], live)
-    angles = length.astype(F32) * held["frequency"][...]
+    angles = length.astype(F32) * frequency_ref[...]
     sine = jnp.sin(angles)
     table_ref[:, :HEAD_SIZE] = jnp.cos(angles)
     table_ref[:, HEAD_SIZE : 2 * HEAD_SIZE] = jnp.where(lane < HEAD_SIZE // 2, -sine, sine)
     table_ref[:, 2 * HEAD_SIZE :] = live.astype(F32)
-
-    for name in ("hidden", "gain"):
-        copies[name].wait()
-    hidden = held["hidden"][...].astype(F32)
-    outputs["hidden"][...] = hidden
-    scaled = (hidden * held["gain"][...]).astype(BF16)
-    squares = jnp.sum(hidden * hidden, axis=1, keepdims=True)
-    squares = jnp.broadcast_to(squares, (requests, HEAD_SIZE))
-    at = 0
-    for name in ("w_query", "w_key", "w_value"):
-        copies[name].wait()
-        part = jnp.dot(scaled, held[name][0], preferred_element_type=F32)
-        width = part.shape[1]
-        for peer in range(out_ref.shape[0]):
-            out_ref[peer, :, at : at + width] = part
-        at += width
-    for peer in range(out_ref.shape[0]):
-        out_ref[peer, :, at:] = squares
-    for name in ("keys", "values", "w_out"):
-        copies[name].wait()
 
 
 def attend(model_width, parts_ref, table_ref, keys_ref, values_ref, out_ref):
@@ -205,6 +171,13 @@
     requests, width = hidden.shape
     ctx_count = lax.axis_size(CTX)
     packed_width = w_query.shape[2] + 2 * key_weight.shape[2] + HEAD_SIZE
+    w_rows = w_out[0]
+    half_columns = w_rows.shape[1] // 2
+    far = lax.axis_index("far")
+    w_kept = lax.dynamic_slice_in_dim(w_rows, far * half_columns, half_columns, 1)
+    w_sent = lax.dynamic_slice_in_dim(w_rows, (1 - far) * half_columns, half_columns, 1)
+    hidden, w_sent = lax.optimization_barrier((hidden, w_sent))
+    w_swapped = from_behind(w_sent, "far", 1)
     sources = (
         lengths,
         jnp.transpose(plan, (1, 2, 0)),
@@ -214,35 +187,18 @@
         w_query,
         key_weight,
         value_weight,
-        key_cache_slots,
-        value_cache_slots,
-        w_out,
     )
-    moved = sources[-3:]
-    parts, table, hidden_f, keys, values, w_out = pl.pallas_call(
+    parts, table, hidden_f = pl.pallas_call(
         project,
         out_shape=(
             pltpu.VMEM((ctx_count, requests, packed_width), F32),
             pltpu.VMEM((requests, 3 * HEAD_SIZE), F32),
             pltpu.VMEM((requests, width), F32),
-        )
-        + tuple(pltpu.VMEM(source.shape, source.dtype) for source in moved),
-        in_specs=[whole(pltpu.HBM)] * len(sources),
-        out_specs=(whole(),) * 6,
-        scratch_shapes=[
-            (pltpu.SMEM if source.dtype == jnp.int32 else pltpu.VMEM)(source.shape, source.dtype)
-            for source in sources[:-3]
-        ]
-        + [pltpu.SemaphoreType.DMA((len(sources),))],
+        ),
+        in_specs=[whole(pltpu.SMEM)] * 2 + [whole()] * 6,
+        out_specs=(whole(),) * 3,
         name="project",
-        compiler_params=pltpu.CompilerParams(vmem_limit_bytes=16 * 2**20),
-    )(*[pltpu.with_memory_space_constraint(source, pltpu.HBM) for source in sources])
-    parts, w_rows = lax.optimization_barrier((parts, w_out[0]))
-    half_columns = w_rows.shape[1] // 2
-    far = lax.axis_index("far")
-    w_kept = lax.dynamic_slice_in_dim(w_rows, far * half_columns, half_columns, 1)
-    w_sent = lax.dynamic_slice_in_dim(w_rows, (1 - far) * half_columns, half_columns, 1)
-    w_swapped = from_behind(w_sent, "far", 1)
+    )(*sources)
     parts = lax.all_to_all(parts, CTX, 0, 0, tiled=True)
     spans = pl.pallas_call(
         functools.partial(attend, width * ctx_count),
@@ -251,7 +207,7 @@
         out_specs=whole(),
         name="attend",
         compiler_params=pltpu.CompilerParams(vmem_limit_bytes=16 * 2**20),
-    )(in_vmem(parts), in_vmem(table), in_vmem(keys), in_vmem(values))
+    )(in_vmem(parts), in_vmem(table), key_cache_slots, value_cache_slots)
     spans = lax.all_to_all(spans, CTX, 0, 0, tiled=True)
     pieces = pl.pallas_call(
         merge_and_project,

time: 54.5 us -> 53.9 us (0.989)
  blocking collectives: 37.8 us -> 36.6 us
  local copies, waits for them, and re-layouts: 0.05 us -> 1.23 us
  Pallas kernels: 3.32 us -> 2.63 us
    dynamic_slice x1, local copies, waits for them, and re-layouts: 0.05 us -> 1.21 us  [per_device(): lax.dynamic_slice_in_dim(w_rows, far * half_columns, half_columns, 1)]
    all_to_all x1, blocking collectives: 16.8 us -> 15.7 us  [per_device(): pieces = lax.all_to_all(pieces, LAST, 0, 0, tiled=True)]
    pallas_call x1, Pallas kernels: 2.06 us -> 1.37 us  [per_device(): pl.pallas_call(project, out_shape=(pltpu.VMEM((ctx_count, requests, packe...]
  transfers between devices with their start and end apart: 2 -> 2, of which waited for: 1 -> 1; matrix products, arithmetic and copies ran while one was open for 1% -> 1% of each run, Pallas kernels for 2% -> 4%
where the time goes in v4:
time: 53.9 us; the launch traced here: 53.6 us
  blocking collectives  36.6 us (68%)
  starting transfers between devices  8.69 us (16%)
  Pallas kernels  2.63 us (5%)
  waiting for transfers between devices  2.2 us (4%)
  local copies, waits for them, and re-layouts  1.23 us (2%)
  matrix products  0.78 us (1%)
  other arithmetic  0.75 us (1%)
  between operations  0.69 us (1%)
    all_to_all x1, blocking collectives, per_device(): pieces = lax.all_to_all(pieces, LAST, 0, 0, tiled=True)  15.7 us
    all_to_all x1, blocking collectives, per_device(): parts = lax.all_to_all(parts, CTX, 0, 0, tiled=True)  13 us
    ppermute x2, starting transfers between devices, from_behind(): lax.ppermute(value, axis, [(source, (source + steps) % count) for source...  8.69 us
    all_to_all x1, blocking collectives, per_device(): spans = lax.all_to_all(spans, CTX, 0, 0, tiled=True)  7.92 us
    ppermute x2, waiting for transfers between devices, from_behind(): lax.ppermute(value, axis, [(source, (source + steps) % count) for source...  2.2 us
    pallas_call x1, Pallas kernels, per_device(): pl.pallas_call(project, out_shape=(pltpu.VMEM((ctx_count, requests, packe...  1.37 us
    dynamic_slice x1, local copies, waits for them, and re-layouts, per_device(): lax.dynamic_slice_in_dim(w_rows, far * half_columns, half_columns, 1)  1.21 us
  transfers between devices with their start and end apart: 2, of which 1 were waited for; matrix products, arithmetic and copies ran while one was open for 1% of the time, Pallas kernels for 4%

profile of v4, /device:TPU:1, one launch (start us, length us, event | category | flops | bytes accessed | tf_op | source)
XLA Modules:
  0.0 53.6 jit_solution(15729066882826518306)
XLA Ops:
  0.6 0.0 copy-start.1
  0.6 0.0 copy-start
  0.7 1.2 %dynamic-slice_bitcast_fusion = (bf16[64,2048]{1,0:T(8,128)(2,1)S(1)}, bf16[64,2048]{1,0:T(8,128)(2,1)S(1)}) fusion(bf16[1,64,4096]{2,1,0:T(8,128)(2,1)} %param.17, s32[]{:T(128)S(6)} %select_n.7, s32[]{:T(128)S(6)} %select_n.6), kind=kLoop, calls=%fused_computation.3 | loop fusion | bytes 1048584 | tf_op jit(solution)/shard_map/dynamic_slice | solution.py:177
  1.9 5.5 %collective-permute-start = (bf16[64,2048]{1,0:T(8,128)(2,1)S(1)}, bf16[64,2048]{1,0:T(8,128)(2,1)S(1)}, u32[]{:S(2)}, u32[]{:S(2)}) collective-permute-start(bf16[64,2048]{1,0:T(8,128)(2,1)S(1)} %get-tuple-element.13), channel_id=1, source_target_pairs={{0,4},{4,0},{1,5},{5,1},{2,6},{6,2},{3,7},{7,3},{8,12},{12,8},{9,1... | collective-permute-start | bytes 786440 | tf_op jit(solution)/shard_map/ppermute | solution.py:149
  7.4 1.4 %project.1 = (f32[8,4,896]{2,1,0:T(4,128)S(1)}, f32[4,384]{1,0:T(4,128)S(1)}, f32[4,512]{1,0:T(4,128)S(1)}) custom-call(s32[4]{0:T(128)} %lengths_ref.1, s32[1,2,4]{2,1,0:T(2,128)} %bitcast.7, f32[1,128]{1,0:T(1,128)} %constant.20.clone.frequency_ref, bf16[4,512]{1,0:T(4,128)(2,1)} %hidden_ref, f32[1,512]{1,0:T(1,128)} %gain_ref.1, ...), custom_call_target="tpu_custom_call" | custom-call | tf_op jit(solution)/shard_map/project/pallas_call | solution.py:191
  8.7 13.0 %all_to_all.15.parts_ref = f32[8,4,896]{2,1,0:T(4,128)S(1)} all-to-all(f32[8,4,896]{2,1,0:T(4,128)S(1)} %get-tuple-element.11), channel_id=1, replica_groups=mesh['section'=8,'tp'=8,'far'=2,'near'=2,'core'=2] {'far','near','core'}, dimensions={0} | all-to-all | bytes 229376 | tf_op jit(solution)/shard_map/all_to_all | solution.py:202
  21.8 0.0 copy-done.1
  21.8 0.0 copy-done
  21.8 0.9 %attend.1 = f32[8,8,128]{2,1,0:T(8,128)S(1)} custom-call(f32[8,4,896]{2,1,0:T(4,128)S(1)} %all_to_all.15.parts_ref, f32[4,384]{1,0:T(4,128)S(1)} %get-tuple-element.12.table_ref, bf16[4,1024,128]{2,1,0:T(8,128)(2,1)S(1)} %copy-done, bf16[4,1024,128]{2,1,0:T(8,128)(2,1)S(1)} %copy-done.1), custom_call_target="tpu_custom_call" | custom-call | tf_op jit(solution)/shard_map/attend/pallas_call | solution.py:203
  22.7 7.9 %all_to_all.16.parts_ref = f32[8,8,128]{2,1,0:T(8,128)S(1)} all-to-all(f32[8,8,128]{2,1,0:T(8,128)S(1)} %attend.1), channel_id=1, replica_groups=mesh['section'=8,'tp'=8,'far'=2,'near'=2,'core'=2] {'far','near','core'}, dimensions={0} | all-to-all | bytes 65536 | tf_op jit(solution)/shard_map/all_to_all | solution.py:211
  30.6 0.0 collective-permute-done.swapped_ref
  30.6 0.3 merge_and_project.1
  31.0 15.7 %all_to_all.17 = bf16[32,4,512]{2,1,0:T(4,128)(2,1)S(1)} all-to-all(bf16[32,4,512]{2,1,0:T(4,128)(2,1)S(1)} %merge_and_project.1), channel_id=1, replica_groups=mesh['section'=8,'tp'=8,'far'=2,'near'=2,'core'=2] {'tp','near','core'}, dimensions={0} | all-to-all | bytes 262144 | tf_op jit(solution)/shard_map/all_to_all | solution.py:219
  46.7 0.1 convert_reduce_fusion.1
  46.7 3.2 %collective-permute-start.1 = (bf16[4,512]{1,0:T(4,128)(2,1)S(1)}, bf16[4,512]{1,0:T(4,128)(2,1)S(1)}, u32[]{:S(2)}, u32[]{:S(2)}) collective-permute-start(bf16[4,512]{1,0:T(4,128)(2,1)S(1)} %add_convert_fusion), channel_id=1, source_target_pairs={{0,64},{64,128},{128,192},{192,256},{256,320},{320,384},{384,448},... | collective-permute-start | bytes 12296 | tf_op jit(solution)/shard_map/ppermute | solution.py:149
  50.0 0.7 %convert_reduce_fusion = f32[4,512]{1,0:T(4,128)} fusion(bf16[32,4,512]{2,1,0:T(4,128)(2,1)S(1)} %all_to_all.17), kind=kLoop, calls=%fused_computation.1 | loop fusion | flops 129024 | bytes 139264 | tf_op jit(solution)/shard_map/reduce_sum | solution.py:223
  50.6 0.0 copy-start.2
  50.6 2.2 %collective-permute-done.1 = bf16[4,512]{1,0:T(4,128)(2,1)S(1)} collective-permute-done((bf16[4,512]{1,0:T(4,128)(2,1)S(1)}, bf16[4,512]{1,0:T(4,128)(2,1)S(1)}, u32[]{:S(2)}, u32[]{:S(2)}) %collective-permute-start.1) | collective-permute-done | bytes 4128 | tf_op jit(solution)/shard_map/ppermute | solution.py:149
  52.8 0.0 copy-done.2
  52.8 0.8 %convolution_convert_fusion = bf16[4,512]{1,0:T(4,128)(2,1)} fusion(bf16[4,512]{1,0:T(4,128)(2,1)S(1)} %collective-permute-done.1, s32[4]{0:T(128)S(1)} %bitcast.8), kind=kOutput, calls=%fused_computation | convolution fusion | flops 18448 | bytes 8208 | tf_op jit(solution)/shard_map/dot_general | solution.py:225
  (1 shorter events, 0.0 us)
Async XLA Ops:
  0.6 21.1 %copy-start.1 = (bf16[4,1024,128]{2,1,0:T(8,128)(2,1)S(1)}, bf16[4,1024,128]{2,1,0:T(8,128)(2,1)}, u32[]{:S(2)}) copy-start(bf16[4,1024,128]{2,1,0:T(8,128)(2,1)} %values_ref.1) | copy-start | bytes 3145732
  0.6 21.1 %copy-start = (bf16[4,1024,128]{2,1,0:T(8,128)(2,1)S(1)}, bf16[4,1024,128]{2,1,0:T(8,128)(2,1)}, u32[]{:S(2)}) copy-start(bf16[4,1024,128]{2,1,0:T(8,128)(2,1)} %keys_ref.1) | copy-start | bytes 3145732
  1.9 28.7 %collective-permute-start = (bf16[64,2048]{1,0:T(8,128)(2,1)S(1)}, bf16[64,2048]{1,0:T(8,128)(2,1)S(1)}, u32[]{:S(2)}, u32[]{:S(2)}) collective-permute-start(bf16[64,2048]{1,0:T(8,128)(2,1)S(1)} %get-tuple-element.13), channel_id=1, source_target_pairs={{0,4},{4,0},{1,5},{5,1},{2,6},{6,2},{3,7},{7,3},{8,12},{12,8},{9,1... | collective-permute-start | bytes 786440 | tf_op jit(solution)/shard_map/ppermute | solution.py:149
  46.7 6.1 %collective-permute-start.1 = (bf16[4,512]{1,0:T(4,128)(2,1)S(1)}, bf16[4,512]{1,0:T(4,128)(2,1)S(1)}, u32[]{:S(2)}, u32[]{:S(2)}) collective-permute-start(bf16[4,512]{1,0:T(4,128)(2,1)S(1)} %add_convert_fusion), channel_id=1, source_target_pairs={{0,64},{64,128},{128,192},{192,256},{256,320},{320,384},{384,448},... | collective-permute-start | bytes 12296 | tf_op jit(solution)/shard_map/ppermute | solution.py:149
  50.6 2.2 %copy-start.2 = (s32[1,4]{1,0:T(1,128)S(1)}, s32[1,4]{1,0:T(1,128)}, u32[]{:S(2)}) copy-start(s32[1,4]{1,0:T(1,128)} %param.22) | copy-start | bytes 52

commit v5 on v4

--- a/solution.py
+++ b/solution.py
@@ -13,8 +13,31 @@
 NEGATIVE = -1e30
 ROPE_BASE = 500000.0
 CTX = ("far", "near", "core")
-LAST = ("tp", "near", "core")
+LAST = ("tp", "far", "near")
+CHIPS = 4
 SCALE = HEAD_SIZE ** (-0.5)
+FETCH_INPUTS = (
+    "lengths",
+    "plan",
+    "frequency",
+    "gain",
+    "hidden",
+    "w_query",
+    "w_key",
+    "w_value",
+    "w_out",
+)
+FETCH_OUTPUTS = (
+    "hidden",
+    "scaled",
+    "squares",
+    "table",
+    "w_query",
+    "w_key",
+    "w_value",
+    "w_sent",
+    "w_kept",
+)
 F32 = jnp.float32
 BF16 = jnp.bfloat16
 
@@ -27,26 +50,34 @@
     return pltpu.with_memory_space_constraint(value, pltpu.VMEM)
 
 
-def project(
-    lengths_ref, plan_ref, frequency_ref, hidden_ref, gain_ref, query_ref, key_ref, value_ref,
-    out_ref, table_ref, hidden_out_ref,
-):
-    hidden = hidden_ref[...].astype(F32)
+def fetch(*refs):
+    count = len(FETCH_INPUTS)
+    outputs = dict(zip(FETCH_OUTPUTS, refs[count:]))
+    lengths_ref, plan_ref, frequency_ref, gain_ref, semaphores = refs[count + len(FETCH_OUTPUTS) :]
+    held = dict(outputs, lengths=lengths_ref, plan=plan_ref, frequency=frequency_ref, gain=gain_ref)
+    sources = dict(zip(FETCH_INPUTS, refs))
+    w_ref = sources.pop("w_out")
+    core, width = lax.axis_index("core"), outputs["w_kept"].shape[1] // CHIPS
+    for name, whose in (("w_sent", 1 - core), ("w_kept", core)):
+        for chip in range(CHIPS):
+            start = pl.multiple_of((2 * chip + whose) * width, HEAD_SIZE)
+            at = pl.ds(chip * width, width)
+            sources[name, chip] = w_ref.at[0, :, pl.ds(start, width)]
+            held[name, chip] = outputs[name].at[:, at]
+    copies = {
+        name: pltpu.make_async_copy(source, held[name], semaphores.at[at])
+        for at, (name, source) in enumerate(sources.items())
+    }
+    for copy in copies.values():
+        copy.start()
+
+    for name in ("lengths", "plan", "frequency", "hidden", "gain"):
+        copies[name].wait()
+    hidden = held["hidden"][...].astype(F32)
     requests = hidden.shape[0]
-    hidden_out_ref[...] = hidden
-    scaled = (hidden * gain_ref[...]).astype(BF16)
+    outputs["scaled"][...] = (hidden * gain_ref[...]).astype(BF16)
     squares = jnp.sum(hidden * hidden, axis=1, keepdims=True)
-    squares = jnp.broadcast_to(squares, (requests, HEAD_SIZE))
-    at = 0
-    for ref in (query_ref, key_ref, value_ref):
-        part = jnp.dot(scaled, ref[0], preferred_element_type=F32)
-        width = part.shape[1]
-        for peer in range(out_ref.shape[0]):
-            out_ref[peer, :, at : at + width] = part
-        at += width
-    for peer in range(out_ref.shape[0]):
-        out_ref[peer, :, at:] = squares
-
+    outputs["squares"][...] = jnp.broadcast_to(squares, (requests, HEAD_SIZE))
     row = lax.broadcasted_iota(jnp.int32, (requests, HEAD_SIZE), 0)
     lane = lax.broadcasted_iota(jnp.int32, (requests, HEAD_SIZE), 1)
     length = jnp.zeros((requests, HEAD_SIZE), jnp.int32)
@@ -56,9 +87,30 @@
         live = jnp.where(row == request, plan_ref[0, 1, request] - plan_ref[0, 0, request], live)
     angles = length.astype(F32) * frequency_ref[...]
     sine = jnp.sin(angles)
+    table_ref = outputs["table"]
     table_ref[:, :HEAD_SIZE] = jnp.cos(angles)
     table_ref[:, HEAD_SIZE : 2 * HEAD_SIZE] = jnp.where(lane < HEAD_SIZE // 2, -sine, sine)
     table_ref[:, 2 * HEAD_SIZE :] = live.astype(F32)
+    for name in ("w_query", "w_key", "w_value"):
+        copies.pop(name).wait()
+    for name in ("lengths", "plan", "frequency", "hidden", "gain"):
+        copies.pop(name)
+    for copy in copies.values():
+        copy.wait()
+
+
+def project(scaled_ref, squares_ref, query_ref, key_ref, value_ref, out_ref):
+    scaled = scaled_ref[...]
+    at = 0
+    for ref in (query_ref, key_ref, value_ref):
+        part = jnp.dot(scaled, ref[0], preferred_element_type=F32)
+        width = part.shape[1]
+        for peer in range(out_ref.shape[0]):
+            out_ref[peer, :, at : at + width] = part
+        at += width
+    squares = squares_ref[...]
+    for peer in range(out_ref.shape[0]):
+        out_ref[peer, :, at:] = squares
 
 
 def attend(model_width, parts_ref, table_ref, keys_ref, values_ref, out_ref):
@@ -113,30 +165,28 @@
     block_out = block_out * factor + new_factor * new_value
 
     lane = lax.broadcasted_iota(jnp.int32, (rows, HEAD_SIZE), 1)
+    statistics = jnp.where(lane == 0, peak, block_sum)
+    for peer in range(out_ref.shape[0]):
+        head = peer // 2
+        own = slice(head * requests, (head + 1) * requests)
+        out_ref[peer, :requests] = block_out[own]
+        out_ref[peer, requests:] = statistics[own]
+
+
+def merge_and_project(parts_ref, kept_ref, swapped_ref, out_ref):
+    peers, requests, width = out_ref.shape
+    statistics = parts_ref[:, requests:]
+    span_max, span_sum = statistics[:, :, :1], statistics[:, :, 1:2]
+    factor = jnp.exp(span_max - jnp.max(span_max, axis=0, keepdims=True))
+    merged = jnp.sum(parts_ref[:, :requests] * factor, axis=0)
+    attended = merged / jnp.sum(span_sum * factor, axis=0)
     half = HEAD_SIZE // 2
-    statistics = jnp.where(lane == half, peak, block_sum)
-    lower = jnp.where(lane < half, block_out, statistics)
-    upper = jnp.where(lane < half, pltpu.roll(block_out, half, 1), statistics)
-    for head in range(heads):
-        for place, source in enumerate((head, head ^ 2)):
-            rows_of = slice(source * requests, (source + 1) * requests)
-            to = slice(place * requests, (place + 1) * requests)
-            out_ref[2 * head, to] = lower[rows_of]
-            out_ref[2 * head + 1, to] = upper[rows_of]
-
-
-def merge_and_project(parts_ref, kept_ref, swapped_ref, out_ref):
-    half = HEAD_SIZE // 2
-    parts = parts_ref[...]
-    span_max = parts[:, :, half : half + 1]
-    peak = jnp.max(span_max, axis=0, keepdims=True)
-    merged = jnp.sum(parts * jnp.exp(span_max - peak), axis=0)
-    attended = merged / merged[:, half + 1 : half + 2]
-    peers, requests, width = out_ref.shape
-    own = attended[:requests, :half].astype(BF16)
-    far = attended[requests:, :half].astype(BF16)
+    lower, upper = attended[:, :half].astype(BF16), attended[:, half:].astype(BF16)
+    first = lax.axis_index("core") == 0
+    own = jnp.where(first, lower, upper)
+    other = jnp.where(first, upper, lower)
     result = jnp.dot(own, kept_ref[...], preferred_element_type=F32)
-    result += jnp.dot(far, swapped_ref[...], preferred_element_type=F32)
+    result += jnp.dot(other, swapped_ref[...], preferred_element_type=F32)
     result = result.astype(BF16)
     columns = result.shape[1] // width
     for peer in range(peers):
@@ -171,34 +221,50 @@
     requests, width = hidden.shape
     ctx_count = lax.axis_size(CTX)
     packed_width = w_query.shape[2] + 2 * key_weight.shape[2] + HEAD_SIZE
-    w_rows = w_out[0]
-    half_columns = w_rows.shape[1] // 2
-    far = lax.axis_index("far")
-    w_kept = lax.dynamic_slice_in_dim(w_rows, far * half_columns, half_columns, 1)
-    w_sent = lax.dynamic_slice_in_dim(w_rows, (1 - far) * half_columns, half_columns, 1)
-    hidden, w_sent = lax.optimization_barrier((hidden, w_sent))
-    w_swapped = from_behind(w_sent, "far", 1)
     sources = (
         lengths,
         jnp.transpose(plan, (1, 2, 0)),
         jnp.asarray(frequencies()),
+        gain,
         hidden,
-        gain,
         w_query,
         key_weight,
         value_weight,
+        w_out,
     )
-    parts, table, hidden_f = pl.pallas_call(
+    half_shape = (w_out.shape[1], w_out.shape[2] // 2)
+    hidden, scaled, squares, table, w_query, key_weight, value_weight, w_sent, w_kept = pl.pallas_call(
+        fetch,
+        out_shape=(
+            pltpu.VMEM(hidden.shape, BF16),
+            pltpu.VMEM(hidden.shape, BF16),
+            pltpu.VMEM((requests, HEAD_SIZE), F32),
+            pltpu.VMEM((requests, 3 * HEAD_SIZE), F32),
+            pltpu.VMEM(w_query.shape, BF16),
+            pltpu.VMEM(key_weight.shape, BF16),
+            pltpu.VMEM(value_weight.shape, BF16),
+            pltpu.VMEM(half_shape, BF16),
+            pltpu.VMEM(half_shape, BF16),
+        ),
+        in_specs=[whole(pltpu.HBM)] * len(FETCH_INPUTS),
+        out_specs=(whole(),) * len(FETCH_OUTPUTS),
+        scratch_shapes=[
+            (pltpu.SMEM if source.dtype == jnp.int32 else pltpu.VMEM)(source.shape, source.dtype)
+            for source in sources[:4]
+        ]
+        + [pltpu.SemaphoreType.DMA((len(sources) - 1 + 2 * CHIPS,))],
+        name="fetch",
+        compiler_params=pltpu.CompilerParams(vmem_limit_bytes=8 * 2**20),
+    )(*[pltpu.with_memory_space_constraint(source, pltpu.HBM) for source in sources])
+    w_swapped = from_behind(w_sent, "core", 1)
+    parts = pl.pallas_call(
         project,
-        out_shape=(
-            pltpu.VMEM((ctx_count, requests, packed_width), F32),
-            pltpu.VMEM((requests, 3 * HEAD_SIZE), F32),
-            pltpu.VMEM((requests, width), F32),
-        ),
-        in_specs=[whole(pltpu.SMEM)] * 2 + [whole()] * 6,
-        out_specs=(whole(),) * 3,
+        out_shape=pltpu.VMEM((ctx_count, requests, packed_width), F32),
+        in_specs=[whole()] * 5,
+        out_specs=whole(),
         name="project",
-    )(*sources)
+        compiler_params=pltpu.CompilerParams(vmem_limit_bytes=8 * 2**20),
+    )(*[in_vmem(value) for value in (scaled, squares, w_query, key_weight, value_weight)])
     parts = lax.all_to_all(parts, CTX, 0, 0, tiled=True)
     spans = pl.pallas_call(
         functools.partial(attend, width * ctx_count),
@@ -206,7 +272,7 @@
         in_specs=[whole()] * 4,
         out_specs=whole(),
         name="attend",
-        compiler_params=pltpu.CompilerParams(vmem_limit_bytes=16 * 2**20),
+        compiler_params=pltpu.CompilerParams(vmem_limit_bytes=8 * 2**20),
     )(in_vmem(parts), in_vmem(table), key_cache_slots, value_cache_slots)
     spans = lax.all_to_all(spans, CTX, 0, 0, tiled=True)
     pieces = pl.pallas_call(
@@ -215,9 +281,10 @@
         in_specs=[whole()] * 3,
         out_specs=whole(),
         name="merge_and_project",
+        compiler_params=pltpu.CompilerParams(vmem_limit_bytes=8 * 2**20),
     )(in_vmem(spans), in_vmem(w_kept), in_vmem(w_swapped))
     pieces = lax.all_to_all(pieces, LAST, 0, 0, tiled=True)
-    section_rows = (hidden_f + pieces.astype(F32).sum(axis=0)).astype(BF16)
+    section_rows = (hidden.astype(F32) + pieces.astype(F32).sum(axis=0)).astype(BF16)
     section_rows, pieces = lax.optimization_barrier((section_rows, pieces))
     arrived = from_behind(section_rows, "section", 1)
     branch_out = pieces.astype(F32).sum(axis=0)

time: 53.9 us -> 53.1 us (0.985)
  the two profiles are of different devices: /device:TPU:1 before, /device:TPU:32 now
where the time goes in v5:
time: 53.1 us; the launch traced here: 52.8 us
  blocking collectives  39.6 us (75%)
  starting transfers between devices  4.5 us (8%)
  waiting for transfers between devices  3.45 us (6%)
  Pallas kernels  3.08 us (6%)
  matrix products  0.78 us (1%)
  other arithmetic  0.75 us (1%)
  between operations  0.69 us (1%)
    all_to_all x1, blocking collectives, per_device(): pieces = lax.all_to_all(pieces, LAST, 0, 0, tiled=True)  21.6 us
    all_to_all x1, blocking collectives, per_device(): parts = lax.all_to_all(parts, CTX, 0, 0, tiled=True)  10.2 us
    all_to_all x1, blocking collectives, per_device(): spans = lax.all_to_all(spans, CTX, 0, 0, tiled=True)  7.82 us
    ppermute x2, starting transfers between devices, from_behind(): lax.ppermute(value, axis, [(source, (source + steps) % count) for source...  4.5 us
    ppermute x2, waiting for transfers between devices, from_behind(): lax.ppermute(value, axis, [(source, (source + steps) % count) for source...  3.45 us
    pallas_call x1, Pallas kernels, per_device(): pl.pallas_call(fetch, out_shape=(pltpu.VMEM(hidden.shape, BF16), pltpu.VM...  1.56 us
  transfers between devices with their start and end apart: 2, of which 1 were waited for; matrix products, arithmetic and copies ran while one was open for 1% of the time, Pallas kernels for 2%

profile of v5, /device:TPU:32, one launch (start us, length us, event | category | flops | bytes accessed | tf_op | source)
XLA Modules:
  0.0 52.8 jit_solution(9639697302657197504)
XLA Ops:
  0.6 0.0 copy-start
  0.6 0.0 copy-start.1
  0.7 1.6 %fetch.1 = (bf16[4,512]{1,0:T(4,128)(2,1)S(1)}, bf16[4,512]{1,0:T(4,128)(2,1)S(1)}, f32[4,128]{1,0:T(4,128)S(1)}, f32[4,384]{1,0:T(4,128)S(1)}, bf16[1,512,512]{...) custom-call(s32[4]{0:T(128)} %refs_0_.1, ...), custom_call_target="tpu_custom_call" | custom-call | tf_op jit(solution)/shard_map/fetch/pallas_call | solution.py:236
  2.2 1.9 %collective-permute-start = (bf16[64,2048]{1,0:T(8,128)(2,1)S(1)}, bf16[64,2048]{1,0:T(8,128)(2,1)S(1)}, u32[]{:S(2)}, u32[]{:S(2)}) collective-permute-start(bf16[64,2048]{1,0:T(8,128)(2,1)S(1)} %get-tuple-element.21), channel_id=1, source_target_pairs={{0,1},{1,0},{2,3},{3,2},{4,5},{5,4},{6,7},{7,6},{8,9},{9,8},{10,11... | collective-permute-start | bytes 786440 | tf_op jit(solution)/shard_map/ppermute | solution.py:199
  4.1 0.2 project.1
  4.4 10.2 %all_to_all.15.parts_ref = f32[8,4,896]{2,1,0:T(4,128)S(1)} all-to-all(f32[8,4,896]{2,1,0:T(4,128)S(1)} %project.1), channel_id=1, replica_groups=mesh['section'=8,'tp'=8,'far'=2,'near'=2,'core'=2] {'far','near','core'}, dimensions={0} | all-to-all | bytes 229376 | tf_op jit(solution)/shard_map/all_to_all | solution.py:268
  14.5 0.0 copy-done
  14.5 0.0 copy-done.1
  14.5 0.8 %attend.1 = f32[8,8,128]{2,1,0:T(8,128)S(1)} custom-call(f32[8,4,896]{2,1,0:T(4,128)S(1)} %all_to_all.15.parts_ref, f32[4,384]{1,0:T(4,128)S(1)} %get-tuple-element.19.table_ref, bf16[4,1024,128]{2,1,0:T(8,128)(2,1)S(1)} %copy-done, bf16[4,1024,128]{2,1,0:T(8,128)(2,1)S(1)} %copy-done.1), custom_call_target="tpu_custom_call" | custom-call | tf_op jit(solution)/shard_map/attend/pallas_call | solution.py:269
  15.4 7.8 %all_to_all.16.parts_ref = f32[8,8,128]{2,1,0:T(8,128)S(1)} all-to-all(f32[8,8,128]{2,1,0:T(8,128)S(1)} %attend.1), channel_id=1, replica_groups=mesh['section'=8,'tp'=8,'far'=2,'near'=2,'core'=2] {'far','near','core'}, dimensions={0} | all-to-all | bytes 65536 | tf_op jit(solution)/shard_map/all_to_all | solution.py:277
  23.2 0.0 collective-permute-done.swapped_ref
  23.2 0.5 merge_and_project.1
  23.7 21.6 %all_to_all.17 = bf16[32,4,512]{2,1,0:T(4,128)(2,1)S(1)} all-to-all(bf16[32,4,512]{2,1,0:T(4,128)(2,1)S(1)} %merge_and_project.1), channel_id=1, replica_groups=mesh['section'=8,'tp'=8,'far'=2,'near'=2,'core'=2] {'tp','far','near'}, dimensions={0} | all-to-all | bytes 262144 | tf_op jit(solution)/shard_map/all_to_all | solution.py:286
  45.3 0.1 convert_reduce_fusion.1
  45.4 2.6 %collective-permute-start.1 = (bf16[4,512]{1,0:T(4,128)(2,1)S(1)}, bf16[4,512]{1,0:T(4,128)(2,1)S(1)}, u32[]{:S(2)}, u32[]{:S(2)}) collective-permute-start(bf16[4,512]{1,0:T(4,128)(2,1)S(1)} %add_convert_fusion), channel_id=1, source_target_pairs={{0,64},{64,128},{128,192},{192,256},{256,320},{320,384},{384,448},... | collective-permute-start | bytes 12296 | tf_op jit(solution)/shard_map/ppermute | solution.py:199
  47.9 0.7 %convert_reduce_fusion = f32[4,512]{1,0:T(4,128)} fusion(bf16[32,4,512]{2,1,0:T(4,128)(2,1)S(1)} %all_to_all.17), kind=kLoop, calls=%fused_computation.1 | loop fusion | flops 129024 | bytes 139264 | tf_op jit(solution)/shard_map/reduce_sum | solution.py:290
  48.6 0.0 copy-start.2
  48.6 3.4 %collective-permute-done.1 = bf16[4,512]{1,0:T(4,128)(2,1)S(1)} collective-permute-done((bf16[4,512]{1,0:T(4,128)(2,1)S(1)}, bf16[4,512]{1,0:T(4,128)(2,1)S(1)}, u32[]{:S(2)}, u32[]{:S(2)}) %collective-permute-start.1) | collective-permute-done | bytes 4128 | tf_op jit(solution)/shard_map/ppermute | solution.py:199
  52.1 0.0 copy-done.2
  52.1 0.8 %convolution_convert_fusion = bf16[4,512]{1,0:T(4,128)(2,1)} fusion(bf16[4,512]{1,0:T(4,128)(2,1)S(1)} %collective-permute-done.1, s32[4]{0:T(128)S(1)} %bitcast.4), kind=kOutput, calls=%fused_computation | convolution fusion | flops 18448 | bytes 8208 | tf_op jit(solution)/shard_map/dot_general | solution.py:292
  (1 shorter events, 0.0 us)
Async XLA Ops:
  0.6 13.9 %copy-start = (bf16[4,1024,128]{2,1,0:T(8,128)(2,1)S(1)}, bf16[4,1024,128]{2,1,0:T(8,128)(2,1)}, u32[]{:S(2)}) copy-start(bf16[4,1024,128]{2,1,0:T(8,128)(2,1)} %keys_ref.1) | copy-start | bytes 3145732
  0.6 13.9 %copy-start.1 = (bf16[4,1024,128]{2,1,0:T(8,128)(2,1)S(1)}, bf16[4,1024,128]{2,1,0:T(8,128)(2,1)}, u32[]{:S(2)}) copy-start(bf16[4,1024,128]{2,1,0:T(8,128)(2,1)} %values_ref.1) | copy-start | bytes 3145732
  2.2 21.0 %collective-permute-start = (bf16[64,2048]{1,0:T(8,128)(2,1)S(1)}, bf16[64,2048]{1,0:T(8,128)(2,1)S(1)}, u32[]{:S(2)}, u32[]{:S(2)}) collective-permute-start(bf16[64,2048]{1,0:T(8,128)(2,1)S(1)} %get-tuple-element.21), channel_id=1, source_target_pairs={{0,1},{1,0},{2,3},{3,2},{4,5},{5,4},{6,7},{7,6},{8,9},{9,8},{10,11... | collective-permute-start | bytes 786440 | tf_op jit(solution)/shard_map/ppermute | solution.py:199
  45.4 6.7 %collective-permute-start.1 = (bf16[4,512]{1,0:T(4,128)(2,1)S(1)}, bf16[4,512]{1,0:T(4,128)(2,1)S(1)}, u32[]{:S(2)}, u32[]{:S(2)}) collective-permute-start(bf16[4,512]{1,0:T(4,128)(2,1)S(1)} %add_convert_fusion), channel_id=1, source_target_pairs={{0,64},{64,128},{128,192},{192,256},{256,320},{320,384},{384,448},... | collective-permute-start | bytes 12296 | tf_op jit(solution)/shard_map/ppermute | solution.py:199
  48.6 3.4 %copy-start.2 = (s32[1,4]{1,0:T(1,128)S(1)}, s32[1,4]{1,0:T(1,128)}, u32[]{:S(2)}) copy-start(s32[1,4]{1,0:T(1,128)} %param.22) | copy-start | bytes 52

commit v6 on v5

--- a/solution.py
+++ b/solution.py
@@ -19,6 +19,7 @@
 FETCH_INPUTS = (
     "lengths",
     "plan",
+    "routing",
     "frequency",
     "gain",
     "hidden",
@@ -32,6 +33,7 @@
     "scaled",
     "squares",
     "table",
+    "order",
     "w_query",
     "w_key",
     "w_value",
@@ -53,8 +55,9 @@
 def fetch(*refs):
     count = len(FETCH_INPUTS)
     outputs = dict(zip(FETCH_OUTPUTS, refs[count:]))
-    lengths_ref, plan_ref, frequency_ref, gain_ref, semaphores = refs[count + len(FETCH_OUTPUTS) :]
-    held = dict(outputs, lengths=lengths_ref, plan=plan_ref, frequency=frequency_ref, gain=gain_ref)
+    scratch = refs[count + len(FETCH_OUTPUTS) :]
+    lengths_ref, plan_ref, routing_ref, frequency_ref, gain_ref, hidden_ref, semaphores = scratch
+    held = dict(outputs, **dict(zip(FETCH_INPUTS, scratch[:-1])))
     sources = dict(zip(FETCH_INPUTS, refs))
     w_ref = sources.pop("w_out")
     core, width = lax.axis_index("core"), outputs["w_kept"].shape[1] // CHIPS
@@ -71,20 +74,24 @@
     for copy in copies.values():
         copy.start()
 
-    for name in ("lengths", "plan", "frequency", "hidden", "gain"):
+    for name in ("lengths", "plan", "routing", "frequency", "hidden", "gain"):
         copies[name].wait()
-    hidden = held["hidden"][...].astype(F32)
+    hidden = hidden_ref[...].astype(F32)
     requests = hidden.shape[0]
-    outputs["scaled"][...] = (hidden * gain_ref[...]).astype(BF16)
+    outputs["hidden"][...] = hidden
+    outputs["scaled"][...] = (hidden * gain_ref[...]).astype(BF16).astype(F32)
     squares = jnp.sum(hidden * hidden, axis=1, keepdims=True)
     outputs["squares"][...] = jnp.broadcast_to(squares, (requests, HEAD_SIZE))
     row = lax.broadcasted_iota(jnp.int32, (requests, HEAD_SIZE), 0)
     lane = lax.broadcasted_iota(jnp.int32, (requests, HEAD_SIZE), 1)
     length = jnp.zeros((requests, HEAD_SIZE), jnp.int32)
     live = jnp.zeros((requests, HEAD_SIZE), jnp.int32)
+    order = jnp.zeros((requests, HEAD_SIZE), jnp.int32)
     for request in range(requests):
         length = jnp.where(row == request, lengths_ref[request], length)
         live = jnp.where(row == request, plan_ref[0, 1, request] - plan_ref[0, 0, request], live)
+        order = jnp.where(row == request, routing_ref[0, request], order)
+    outputs["order"][...] = order
     angles = length.astype(F32) * frequency_ref[...]
     sine = jnp.sin(angles)
     table_ref = outputs["table"]
@@ -93,14 +100,14 @@
     table_ref[:, 2 * HEAD_SIZE :] = live.astype(F32)
     for name in ("w_query", "w_key", "w_value"):
         copies.pop(name).wait()
-    for name in ("lengths", "plan", "frequency", "hidden", "gain"):
+    for name in ("lengths", "plan", "routing", "frequency", "hidden", "gain"):
         copies.pop(name)
     for copy in copies.values():
         copy.wait()
 
 
 def project(scaled_ref, squares_ref, query_ref, key_ref, value_ref, out_ref):
-    scaled = scaled_ref[...]
+    scaled = scaled_ref[...].astype(BF16)
     at = 0
     for ref in (query_ref, key_ref, value_ref):
         part = jnp.dot(scaled, ref[0], preferred_element_type=F32)
@@ -194,6 +201,15 @@
         out_ref[peer] = result[:, at : at + width]
 
 
+def reorder(arrived_ref, order_ref, out_ref):
+    arrived = arrived_ref[...].astype(F32)
+    order = order_ref[:, :1]
+    result = jnp.zeros_like(arrived)
+    for request in range(arrived.shape[0]):
+        result = jnp.where(order == request, arrived[request : request + 1], result)
+    out_ref[...] = result.astype(BF16)
+
+
 def from_behind(value, axis, steps):
     count = lax.axis_size(axis)
     return lax.ppermute(value, axis, [(source, (source + steps) % count) for source in range(count)])
@@ -224,6 +240,7 @@
     sources = (
         lengths,
         jnp.transpose(plan, (1, 2, 0)),
+        routing,
         jnp.asarray(frequencies()),
         gain,
         hidden,
@@ -233,13 +250,14 @@
         w_out,
     )
     half_shape = (w_out.shape[1], w_out.shape[2] // 2)
-    hidden, scaled, squares, table, w_query, key_weight, value_weight, w_sent, w_kept = pl.pallas_call(
+    hidden, scaled, squares, table, order, w_query, key_weight, value_weight, w_sent, w_kept = pl.pallas_call(
         fetch,
         out_shape=(
-            pltpu.VMEM(hidden.shape, BF16),
-            pltpu.VMEM(hidden.shape, BF16),
+            pltpu.VMEM(hidden.shape, F32),
+            pltpu.VMEM(hidden.shape, F32),
             pltpu.VMEM((requests, HEAD_SIZE), F32),
             pltpu.VMEM((requests, 3 * HEAD_SIZE), F32),
+            pltpu.VMEM((requests, HEAD_SIZE), jnp.int32),
             pltpu.VMEM(w_query.shape, BF16),
             pltpu.VMEM(key_weight.shape, BF16),
             pltpu.VMEM(value_weight.shape, BF16),
@@ -250,7 +268,7 @@
         out_specs=(whole(),) * len(FETCH_OUTPUTS),
         scratch_shapes=[
             (pltpu.SMEM if source.dtype == jnp.int32 else pltpu.VMEM)(source.shape, source.dtype)
-            for source in sources[:4]
+            for source in sources[:6]
         ]
         + [pltpu.SemaphoreType.DMA((len(sources) - 1 + 2 * CHIPS,))],
         name="fetch",
@@ -284,12 +302,18 @@
         compiler_params=pltpu.CompilerParams(vmem_limit_bytes=8 * 2**20),
     )(in_vmem(spans), in_vmem(w_kept), in_vmem(w_swapped))
     pieces = lax.all_to_all(pieces, LAST, 0, 0, tiled=True)
-    section_rows = (hidden.astype(F32) + pieces.astype(F32).sum(axis=0)).astype(BF16)
+    section_rows = (hidden + pieces.astype(F32).sum(axis=0)).astype(BF16)
     section_rows, pieces = lax.optimization_barrier((section_rows, pieces))
     arrived = from_behind(section_rows, "section", 1)
     branch_out = pieces.astype(F32).sum(axis=0)
-    selector = (routing[0][:, None] == jnp.arange(requests, dtype=jnp.int32)[None, :]).astype(BF16)
-    handed = jnp.dot(selector, arrived, preferred_element_type=F32).astype(BF16)
+    handed = pl.pallas_call(
+        reorder,
+        out_shape=jax.ShapeDtypeStruct(arrived.shape, BF16),
+        in_specs=[whole()] * 2,
+        out_specs=whole(),
+        name="reorder",
+        compiler_params=pltpu.CompilerParams(vmem_limit_bytes=8 * 2**20),
+    )(in_vmem(arrived), in_vmem(order))
     return (handed, branch_out)
 
 

time: 53.1 us -> 53 us (level)
  matrix products: 0.78 us -> 0 us
  Pallas kernels: 3.08 us -> 3.76 us
    dot_general x1 -> x0, matrix products: 0.78 us -> none  [per_device(): handed = jnp.dot(selector, arrived, preferred_element_type=F32).astype(BF16)]
    pallas_call x1 -> x2, Pallas kernels: 1.56 us -> 2.24 us  [the longest x1 1.57 us: per_device(): pl.pallas_call(fetch, out_shape=(pltpu.VMEM(hidden.shape, F32), pltpu.VME...]
where the time goes in v6:
time: 53 us; the launch traced here: 52.7 us
  blocking collectives  39.6 us (75%)
  starting transfers between devices  4.51 us (9%)
  Pallas kernels  3.76 us (7%)
  waiting for transfers between devices  3.45 us (7%)
  other arithmetic  0.75 us (1%)
  between operations  0.69 us (1%)
    all_to_all x1, blocking collectives, per_device(): pieces = lax.all_to_all(pieces, LAST, 0, 0, tiled=True)  21.6 us
    all_to_all x1, blocking collectives, per_device(): parts = lax.all_to_all(parts, CTX, 0, 0, tiled=True)  10.2 us
    all_to_all x1, blocking collectives, per_device(): spans = lax.all_to_all(spans, CTX, 0, 0, tiled=True)  7.82 us
    ppermute x2, starting transfers between devices, from_behind(): lax.ppermute(value, axis, [(source, (source + steps) % count) for source...  4.51 us
    ppermute x2, waiting for transfers between devices, from_behind(): lax.ppermute(value, axis, [(source, (source + steps) % count) for source...  3.45 us
    pallas_call x1, Pallas kernels, per_device(): pl.pallas_call(fetch, out_shape=(pltpu.VMEM(hidden.shape, F32), pltpu.VME...  1.57 us
  transfers between devices with their start and end apart: 2, of which 1 were waited for; matrix products, arithmetic and copies ran while one was open for 1% of the time, Pallas kernels for 2%

profile of v6, /device:TPU:32, one launch (start us, length us, event | category | flops | bytes accessed | tf_op | source)
XLA Modules:
  0.0 52.7 jit_solution(17450181798223569584)
XLA Ops:
  0.6 0.0 copy-start
  0.6 0.0 copy-start.1
  0.7 1.6 %fetch.1 = (f32[4,512]{1,0:T(4,128)S(1)}, f32[4,512]{1,0:T(4,128)S(1)}, f32[4,128]{1,0:T(4,128)S(1)}, f32[4,384]{1,0:T(4,128)S(1)}, s32[4,128]{1,0:T(4,128)S(1)}...) custom-call(s32[4]{0:T(128)} %refs_0_.1, ...), custom_call_target="tpu_custom_call" | custom-call | tf_op jit(solution)/shard_map/fetch/pallas_call | solution.py:253
  2.2 1.9 %collective-permute-start = (bf16[64,2048]{1,0:T(8,128)(2,1)S(1)}, bf16[64,2048]{1,0:T(8,128)(2,1)S(1)}, u32[]{:S(2)}, u32[]{:S(2)}) collective-permute-start(bf16[64,2048]{1,0:T(8,128)(2,1)S(1)} %get-tuple-element.22), channel_id=1, source_target_pairs={{0,1},{1,0},{2,3},{3,2},{4,5},{5,4},{6,7},{7,6},{8,9},{9,8},{10,11... | collective-permute-start | bytes 786440 | tf_op jit(solution)/shard_map/ppermute | solution.py:215
  4.2 0.2 project.1
  4.4 10.2 %all_to_all.15.parts_ref = f32[8,4,896]{2,1,0:T(4,128)S(1)} all-to-all(f32[8,4,896]{2,1,0:T(4,128)S(1)} %project.1), channel_id=1, replica_groups=mesh['section'=8,'tp'=8,'far'=2,'near'=2,'core'=2] {'far','near','core'}, dimensions={0} | all-to-all | bytes 229376 | tf_op jit(solution)/shard_map/all_to_all | solution.py:286
  14.5 0.0 copy-done
  14.5 0.0 copy-done.1
  14.5 0.8 %attend.1 = f32[8,8,128]{2,1,0:T(8,128)S(1)} custom-call(f32[8,4,896]{2,1,0:T(4,128)S(1)} %all_to_all.15.parts_ref, f32[4,384]{1,0:T(4,128)S(1)} %get-tuple-element.20.table_ref, bf16[4,1024,128]{2,1,0:T(8,128)(2,1)S(1)} %copy-done, bf16[4,1024,128]{2,1,0:T(8,128)(2,1)S(1)} %copy-done.1), custom_call_target="tpu_custom_call" | custom-call | tf_op jit(solution)/shard_map/attend/pallas_call | solution.py:287
  15.4 7.8 %all_to_all.16.parts_ref = f32[8,8,128]{2,1,0:T(8,128)S(1)} all-to-all(f32[8,8,128]{2,1,0:T(8,128)S(1)} %attend.1), channel_id=1, replica_groups=mesh['section'=8,'tp'=8,'far'=2,'near'=2,'core'=2] {'far','near','core'}, dimensions={0} | all-to-all | bytes 65536 | tf_op jit(solution)/shard_map/all_to_all | solution.py:295
  23.2 0.0 collective-permute-done.swapped_ref
  23.2 0.5 merge_and_project.1
  23.7 21.6 %all_to_all.17 = bf16[32,4,512]{2,1,0:T(4,128)(2,1)S(1)} all-to-all(bf16[32,4,512]{2,1,0:T(4,128)(2,1)S(1)} %merge_and_project.1), channel_id=1, replica_groups=mesh['section'=8,'tp'=8,'far'=2,'near'=2,'core'=2] {'tp','far','near'}, dimensions={0} | all-to-all | bytes 262144 | tf_op jit(solution)/shard_map/all_to_all | solution.py:304
  45.3 0.1 convert_reduce_fusion.1
  45.4 2.6 %collective-permute-start.1 = (bf16[4,512]{1,0:T(4,128)(2,1)S(1)}, bf16[4,512]{1,0:T(4,128)(2,1)S(1)}, u32[]{:S(2)}, u32[]{:S(2)}) collective-permute-start(bf16[4,512]{1,0:T(4,128)(2,1)S(1)} %add_convert_fusion), channel_id=1, source_target_pairs={{0,64},{64,128},{128,192},{192,256},{256,320},{320,384},{384,448},... | collective-permute-start | bytes 12296 | tf_op jit(solution)/shard_map/ppermute | solution.py:215
  48.0 0.7 %convert_reduce_fusion = f32[4,512]{1,0:T(4,128)} fusion(bf16[32,4,512]{2,1,0:T(4,128)(2,1)S(1)} %all_to_all.17), kind=kLoop, calls=%fused_computation | loop fusion | flops 129024 | bytes 139264 | tf_op jit(solution)/shard_map/reduce_sum | solution.py:308
  48.6 3.4 %collective-permute-done.1.arrived_ref = bf16[4,512]{1,0:T(4,128)(2,1)S(1)} collective-permute-done((bf16[4,512]{1,0:T(4,128)(2,1)S(1)}, bf16[4,512]{1,0:T(4,128)(2,1)S(1)}, u32[]{:S(2)}, u32[]{:S(2)}) %collective-permute-start.1) | collective-permute-done | bytes 4128 | tf_op jit(solution)/shard_map/ppermute | solution.py:215
  52.1 0.7 %reorder.1 = bf16[4,512]{1,0:T(4,128)(2,1)} custom-call(bf16[4,512]{1,0:T(4,128)(2,1)S(1)} %collective-permute-done.1.arrived_ref, s32[4,128]{1,0:T(4,128)S(1)} %get-tuple-element.24.order_ref), custom_call_target="tpu_custom_call" | custom-call | tf_op jit(solution)/shard_map/reorder/pallas_call | solution.py:309
  (1 shorter events, 0.0 us)
Async XLA Ops:
  0.6 13.9 %copy-start = (bf16[4,1024,128]{2,1,0:T(8,128)(2,1)S(1)}, bf16[4,1024,128]{2,1,0:T(8,128)(2,1)}, u32[]{:S(2)}) copy-start(bf16[4,1024,128]{2,1,0:T(8,128)(2,1)} %keys_ref.1) | copy-start | bytes 3145732
  0.6 13.9 %copy-start.1 = (bf16[4,1024,128]{2,1,0:T(8,128)(2,1)S(1)}, bf16[4,1024,128]{2,1,0:T(8,128)(2,1)}, u32[]{:S(2)}) copy-start(bf16[4,1024,128]{2,1,0:T(8,128)(2,1)} %values_ref.1) | copy-start | bytes 3145732
  2.2 21.0 %collective-permute-start = (bf16[64,2048]{1,0:T(8,128)(2,1)S(1)}, bf16[64,2048]{1,0:T(8,128)(2,1)S(1)}, u32[]{:S(2)}, u32[]{:S(2)}) collective-permute-start(bf16[64,2048]{1,0:T(8,128)(2,1)S(1)} %get-tuple-element.22), channel_id=1, source_target_pairs={{0,1},{1,0},{2,3},{3,2},{4,5},{5,4},{6,7},{7,6},{8,9},{9,8},{10,11... | collective-permute-start | bytes 786440 | tf_op jit(solution)/shard_map/ppermute | solution.py:215
  45.4 6.7 %collective-permute-start.1 = (bf16[4,512]{1,0:T(4,128)(2,1)S(1)}, bf16[4,512]{1,0:T(4,128)(2,1)S(1)}, u32[]{:S(2)}, u32[]{:S(2)}) collective-permute-start(bf16[4,512]{1,0:T(4,128)(2,1)S(1)} %add_convert_fusion), channel_id=1, source_target_pairs={{0,64},{64,128},{128,192},{192,256},{256,320},{320,384},{384,448},... | collective-permute-start | bytes 12296 | tf_op jit(solution)/shard_map/ppermute | solution.py:215

commit v7 on v5

--- a/solution.py
+++ b/solution.py
@@ -13,7 +13,7 @@
 NEGATIVE = -1e30
 ROPE_BASE = 500000.0
 CTX = ("far", "near", "core")
-LAST = ("tp", "far", "near")
+LAST = ("far", "near", "tp")
 CHIPS = 4
 SCALE = HEAD_SIZE ** (-0.5)
 FETCH_INPUTS = (
@@ -190,7 +190,7 @@
     result = result.astype(BF16)
     columns = result.shape[1] // width
     for peer in range(peers):
-        at = peer % columns * width
+        at = peer // (peers // columns) * width
         out_ref[peer] = result[:, at : at + width]
 
 

time: 53.1 us -> 52.9 us (level)
  no operation moved by 1% of the time
where the time goes in v7:
time: 52.9 us; the launch traced here: 52.6 us
  blocking collectives  39.4 us (74%)
  starting transfers between devices  4.5 us (9%)
  waiting for transfers between devices  3.45 us (7%)
  Pallas kernels  3.08 us (6%)
  matrix products  0.78 us (1%)
  other arithmetic  0.75 us (1%)
  between operations  0.69 us (1%)
    all_to_all x1, blocking collectives, per_device(): pieces = lax.all_to_all(pieces, LAST, 0, 0, tiled=True)  21.4 us
    all_to_all x1, blocking collectives, per_device(): parts = lax.all_to_all(parts, CTX, 0, 0, tiled=True)  10.2 us
    all_to_all x1, blocking collectives, per_device(): spans = lax.all_to_all(spans, CTX, 0, 0, tiled=True)  7.82 us
    ppermute x2, starting transfers between devices, from_behind(): lax.ppermute(value, axis, [(source, (source + steps) % count) for source...  4.5 us
    ppermute x2, waiting for transfers between devices, from_behind(): lax.ppermute(value, axis, [(source, (source + steps) % count) for source...  3.45 us
    pallas_call x1, Pallas kernels, per_device(): pl.pallas_call(fetch, out_shape=(pltpu.VMEM(hidden.shape, BF16), pltpu.VM...  1.56 us
  transfers between devices with their start and end apart: 2, of which 1 were waited for; matrix products, arithmetic and copies ran while one was open for 1% of the time, Pallas kernels for 2%

profile of v7, /device:TPU:32, one launch (start us, length us, event | category | flops | bytes accessed | tf_op | source)
XLA Modules:
  0.0 52.6 jit_solution(4510770956409126606)
XLA Ops:
  0.6 0.0 copy-start
  0.6 0.0 copy-start.1
  0.7 1.6 %fetch.1 = (bf16[4,512]{1,0:T(4,128)(2,1)S(1)}, bf16[4,512]{1,0:T(4,128)(2,1)S(1)}, f32[4,128]{1,0:T(4,128)S(1)}, f32[4,384]{1,0:T(4,128)S(1)}, bf16[1,512,512]{...) custom-call(s32[4]{0:T(128)} %refs_0_.1, ...), custom_call_target="tpu_custom_call" | custom-call | tf_op jit(solution)/shard_map/fetch/pallas_call | solution.py:236
  2.2 1.9 %collective-permute-start = (bf16[64,2048]{1,0:T(8,128)(2,1)S(1)}, bf16[64,2048]{1,0:T(8,128)(2,1)S(1)}, u32[]{:S(2)}, u32[]{:S(2)}) collective-permute-start(bf16[64,2048]{1,0:T(8,128)(2,1)S(1)} %get-tuple-element.21), channel_id=1, source_target_pairs={{0,1},{1,0},{2,3},{3,2},{4,5},{5,4},{6,7},{7,6},{8,9},{9,8},{10,11... | collective-permute-start | bytes 786440 | tf_op jit(solution)/shard_map/ppermute | solution.py:199
  4.1 0.2 project.1
  4.4 10.2 %all_to_all.15.parts_ref = f32[8,4,896]{2,1,0:T(4,128)S(1)} all-to-all(f32[8,4,896]{2,1,0:T(4,128)S(1)} %project.1), channel_id=1, replica_groups=mesh['section'=8,'tp'=8,'far'=2,'near'=2,'core'=2] {'far','near','core'}, dimensions={0} | all-to-all | bytes 229376 | tf_op jit(solution)/shard_map/all_to_all | solution.py:268
  14.5 0.0 copy-done
  14.5 0.0 copy-done.1
  14.5 0.8 %attend.1 = f32[8,8,128]{2,1,0:T(8,128)S(1)} custom-call(f32[8,4,896]{2,1,0:T(4,128)S(1)} %all_to_all.15.parts_ref, f32[4,384]{1,0:T(4,128)S(1)} %get-tuple-element.19.table_ref, bf16[4,1024,128]{2,1,0:T(8,128)(2,1)S(1)} %copy-done, bf16[4,1024,128]{2,1,0:T(8,128)(2,1)S(1)} %copy-done.1), custom_call_target="tpu_custom_call" | custom-call | tf_op jit(solution)/shard_map/attend/pallas_call | solution.py:269
  15.4 7.8 %all_to_all.16.parts_ref = f32[8,8,128]{2,1,0:T(8,128)S(1)} all-to-all(f32[8,8,128]{2,1,0:T(8,128)S(1)} %attend.1), channel_id=1, replica_groups=mesh['section'=8,'tp'=8,'far'=2,'near'=2,'core'=2] {'far','near','core'}, dimensions={0} | all-to-all | bytes 65536 | tf_op jit(solution)/shard_map/all_to_all | solution.py:277
  23.2 0.0 collective-permute-done.swapped_ref
  23.2 0.5 merge_and_project.1
  23.7 21.4 %all_to_all.17 = bf16[32,4,512]{2,1,0:T(4,128)(2,1)S(1)} all-to-all(bf16[32,4,512]{2,1,0:T(4,128)(2,1)S(1)} %merge_and_project.1), channel_id=1, replica_groups=mesh['section'=8,'tp'=8,'far'=2,'near'=2,'core'=2] {'far','near','tp'}, dimensions={0} | all-to-all | bytes 262144 | tf_op jit(solution)/shard_map/all_to_all | solution.py:286
  45.0 0.1 convert_reduce_fusion.1
  45.1 2.6 %collective-permute-start.1 = (bf16[4,512]{1,0:T(4,128)(2,1)S(1)}, bf16[4,512]{1,0:T(4,128)(2,1)S(1)}, u32[]{:S(2)}, u32[]{:S(2)}) collective-permute-start(bf16[4,512]{1,0:T(4,128)(2,1)S(1)} %add_convert_fusion), channel_id=1, source_target_pairs={{0,64},{64,128},{128,192},{192,256},{256,320},{320,384},{384,448},... | collective-permute-start | bytes 12296 | tf_op jit(solution)/shard_map/ppermute | solution.py:199
  47.7 0.7 %convert_reduce_fusion = f32[4,512]{1,0:T(4,128)} fusion(bf16[32,4,512]{2,1,0:T(4,128)(2,1)S(1)} %all_to_all.17), kind=kLoop, calls=%fused_computation.1 | loop fusion | flops 129024 | bytes 139264 | tf_op jit(solution)/shard_map/reduce_sum | solution.py:290
  48.4 0.0 copy-start.2
  48.4 3.4 %collective-permute-done.1 = bf16[4,512]{1,0:T(4,128)(2,1)S(1)} collective-permute-done((bf16[4,512]{1,0:T(4,128)(2,1)S(1)}, bf16[4,512]{1,0:T(4,128)(2,1)S(1)}, u32[]{:S(2)}, u32[]{:S(2)}) %collective-permute-start.1) | collective-permute-done | bytes 4128 | tf_op jit(solution)/shard_map/ppermute | solution.py:199
  51.8 0.0 copy-done.2
  51.8 0.8 %convolution_convert_fusion = bf16[4,512]{1,0:T(4,128)(2,1)} fusion(bf16[4,512]{1,0:T(4,128)(2,1)S(1)} %collective-permute-done.1, s32[4]{0:T(128)S(1)} %bitcast.4), kind=kOutput, calls=%fused_computation | convolution fusion | flops 18448 | bytes 8208 | tf_op jit(solution)/shard_map/dot_general | solution.py:292
  (1 shorter events, 0.0 us)
Async XLA Ops:
  0.6 13.9 %copy-start = (bf16[4,1024,128]{2,1,0:T(8,128)(2,1)S(1)}, bf16[4,1024,128]{2,1,0:T(8,128)(2,1)}, u32[]{:S(2)}) copy-start(bf16[4,1024,128]{2,1,0:T(8,128)(2,1)} %keys_ref.1) | copy-start | bytes 3145732
  0.6 13.9 %copy-start.1 = (bf16[4,1024,128]{2,1,0:T(8,128)(2,1)S(1)}, bf16[4,1024,128]{2,1,0:T(8,128)(2,1)}, u32[]{:S(2)}) copy-start(bf16[4,1024,128]{2,1,0:T(8,128)(2,1)} %values_ref.1) | copy-start | bytes 3145732
  2.2 21.0 %collective-permute-start = (bf16[64,2048]{1,0:T(8,128)(2,1)S(1)}, bf16[64,2048]{1,0:T(8,128)(2,1)S(1)}, u32[]{:S(2)}, u32[]{:S(2)}) collective-permute-start(bf16[64,2048]{1,0:T(8,128)(2,1)S(1)} %get-tuple-element.21), channel_id=1, source_target_pairs={{0,1},{1,0},{2,3},{3,2},{4,5},{5,4},{6,7},{7,6},{8,9},{9,8},{10,11... | collective-permute-start | bytes 786440 | tf_op jit(solution)/shard_map/ppermute | solution.py:199
  45.1 6.7 %collective-permute-start.1 = (bf16[4,512]{1,0:T(4,128)(2,1)S(1)}, bf16[4,512]{1,0:T(4,128)(2,1)S(1)}, u32[]{:S(2)}, u32[]{:S(2)}) collective-permute-start(bf16[4,512]{1,0:T(4,128)(2,1)S(1)} %add_convert_fusion), channel_id=1, source_target_pairs={{0,64},{64,128},{128,192},{192,256},{256,320},{320,384},{384,448},... | collective-permute-start | bytes 12296 | tf_op jit(solution)/shard_map/ppermute | solution.py:199
  48.4 3.4 %copy-start.2 = (s32[1,4]{1,0:T(1,128)S(1)}, s32[1,4]{1,0:T(1,128)}, u32[]{:S(2)}) copy-start(s32[1,4]{1,0:T(1,128)} %param.22) | copy-start | bytes 52

commit v8 on v6

--- a/solution.py
+++ b/solution.py
@@ -13,7 +13,7 @@
 NEGATIVE = -1e30
 ROPE_BASE = 500000.0
 CTX = ("far", "near", "core")
-LAST = ("tp", "far", "near")
+LAST = ("far", "near", "tp")
 CHIPS = 4
 SCALE = HEAD_SIZE ** (-0.5)
 FETCH_INPUTS = (
@@ -197,7 +197,7 @@
     result = result.astype(BF16)
     columns = result.shape[1] // width
     for peer in range(peers):
-        at = peer % columns * width
+        at = peer // (peers // columns) * width
         out_ref[peer] = result[:, at : at + width]
 
 

time: 53 us -> 52.8 us (level)
  no operation moved by 1% of the time
where the time goes in v8:
time: 52.8 us; the launch traced here: 52.5 us
  blocking collectives  39.4 us (75%)
  starting transfers between devices  4.51 us (9%)
  Pallas kernels  3.76 us (7%)
  waiting for transfers between devices  3.45 us (7%)
  other arithmetic  0.75 us (1%)
  between operations  0.69 us (1%)
    all_to_all x1, blocking collectives, per_device(): pieces = lax.all_to_all(pieces, LAST, 0, 0, tiled=True)  21.4 us
    all_to_all x1, blocking collectives, per_device(): parts = lax.all_to_all(parts, CTX, 0, 0, tiled=True)  10.2 us
    all_to_all x1, blocking collectives, per_device(): spans = lax.all_to_all(spans, CTX, 0, 0, tiled=True)  7.82 us
    ppermute x2, starting transfers between devices, from_behind(): lax.ppermute(value, axis, [(source, (source + steps) % count) for source...  4.51 us
    ppermute x2, waiting for transfers between devices, from_behind(): lax.ppermute(value, axis, [(source, (source + steps) % count) for source...  3.45 us
    pallas_call x1, Pallas kernels, per_device(): pl.pallas_call(fetch, out_shape=(pltpu.VMEM(hidden.shape, F32), pltpu.VME...  1.57 us
  transfers between devices with their start and end apart: 2, of which 1 were waited for; matrix products, arithmetic and copies ran while one was open for 1% of the time, Pallas kernels for 2%

profile of v8, /device:TPU:32, one launch (start us, length us, event | category | flops | bytes accessed | tf_op | source)
XLA Modules:
  0.0 52.5 jit_solution(14115209648110337522)
XLA Ops:
  0.6 0.0 copy-start
  0.6 0.0 copy-start.1
  0.7 1.6 %fetch.1 = (f32[4,512]{1,0:T(4,128)S(1)}, f32[4,512]{1,0:T(4,128)S(1)}, f32[4,128]{1,0:T(4,128)S(1)}, f32[4,384]{1,0:T(4,128)S(1)}, s32[4,128]{1,0:T(4,128)S(1)}...) custom-call(s32[4]{0:T(128)} %refs_0_.1, ...), custom_call_target="tpu_custom_call" | custom-call | tf_op jit(solution)/shard_map/fetch/pallas_call | solution.py:253
  2.2 1.9 %collective-permute-start = (bf16[64,2048]{1,0:T(8,128)(2,1)S(1)}, bf16[64,2048]{1,0:T(8,128)(2,1)S(1)}, u32[]{:S(2)}, u32[]{:S(2)}) collective-permute-start(bf16[64,2048]{1,0:T(8,128)(2,1)S(1)} %get-tuple-element.22), channel_id=1, source_target_pairs={{0,1},{1,0},{2,3},{3,2},{4,5},{5,4},{6,7},{7,6},{8,9},{9,8},{10,11... | collective-permute-start | bytes 786440 | tf_op jit(solution)/shard_map/ppermute | solution.py:215
  4.2 0.2 project.1
  4.4 10.2 %all_to_all.15.parts_ref = f32[8,4,896]{2,1,0:T(4,128)S(1)} all-to-all(f32[8,4,896]{2,1,0:T(4,128)S(1)} %project.1), channel_id=1, replica_groups=mesh['section'=8,'tp'=8,'far'=2,'near'=2,'core'=2] {'far','near','core'}, dimensions={0} | all-to-all | bytes 229376 | tf_op jit(solution)/shard_map/all_to_all | solution.py:286
  14.5 0.0 copy-done
  14.5 0.0 copy-done.1
  14.5 0.8 %attend.1 = f32[8,8,128]{2,1,0:T(8,128)S(1)} custom-call(f32[8,4,896]{2,1,0:T(4,128)S(1)} %all_to_all.15.parts_ref, f32[4,384]{1,0:T(4,128)S(1)} %get-tuple-element.20.table_ref, bf16[4,1024,128]{2,1,0:T(8,128)(2,1)S(1)} %copy-done, bf16[4,1024,128]{2,1,0:T(8,128)(2,1)S(1)} %copy-done.1), custom_call_target="tpu_custom_call" | custom-call | tf_op jit(solution)/shard_map/attend/pallas_call | solution.py:287
  15.4 7.8 %all_to_all.16.parts_ref = f32[8,8,128]{2,1,0:T(8,128)S(1)} all-to-all(f32[8,8,128]{2,1,0:T(8,128)S(1)} %attend.1), channel_id=1, replica_groups=mesh['section'=8,'tp'=8,'far'=2,'near'=2,'core'=2] {'far','near','core'}, dimensions={0} | all-to-all | bytes 65536 | tf_op jit(solution)/shard_map/all_to_all | solution.py:295
  23.2 0.0 collective-permute-done.swapped_ref
  23.2 0.5 merge_and_project.1
  23.7 21.4 %all_to_all.17 = bf16[32,4,512]{2,1,0:T(4,128)(2,1)S(1)} all-to-all(bf16[32,4,512]{2,1,0:T(4,128)(2,1)S(1)} %merge_and_project.1), channel_id=1, replica_groups=mesh['section'=8,'tp'=8,'far'=2,'near'=2,'core'=2] {'far','near','tp'}, dimensions={0} | all-to-all | bytes 262144 | tf_op jit(solution)/shard_map/all_to_all | solution.py:304
  45.1 0.1 convert_reduce_fusion.1
  45.1 2.6 %collective-permute-start.1 = (bf16[4,512]{1,0:T(4,128)(2,1)S(1)}, bf16[4,512]{1,0:T(4,128)(2,1)S(1)}, u32[]{:S(2)}, u32[]{:S(2)}) collective-permute-start(bf16[4,512]{1,0:T(4,128)(2,1)S(1)} %add_convert_fusion), channel_id=1, source_target_pairs={{0,64},{64,128},{128,192},{192,256},{256,320},{320,384},{384,448},... | collective-permute-start | bytes 12296 | tf_op jit(solution)/shard_map/ppermute | solution.py:215
  47.7 0.7 %convert_reduce_fusion = f32[4,512]{1,0:T(4,128)} fusion(bf16[32,4,512]{2,1,0:T(4,128)(2,1)S(1)} %all_to_all.17), kind=kLoop, calls=%fused_computation | loop fusion | flops 129024 | bytes 139264 | tf_op jit(solution)/shard_map/reduce_sum | solution.py:308
  48.4 3.4 %collective-permute-done.1.arrived_ref = bf16[4,512]{1,0:T(4,128)(2,1)S(1)} collective-permute-done((bf16[4,512]{1,0:T(4,128)(2,1)S(1)}, bf16[4,512]{1,0:T(4,128)(2,1)S(1)}, u32[]{:S(2)}, u32[]{:S(2)}) %collective-permute-start.1) | collective-permute-done | bytes 4128 | tf_op jit(solution)/shard_map/ppermute | solution.py:215
  51.9 0.7 %reorder.1 = bf16[4,512]{1,0:T(4,128)(2,1)} custom-call(bf16[4,512]{1,0:T(4,128)(2,1)S(1)} %collective-permute-done.1.arrived_ref, s32[4,128]{1,0:T(4,128)S(1)} %get-tuple-element.24.order_ref), custom_call_target="tpu_custom_call" | custom-call | tf_op jit(solution)/shard_map/reorder/pallas_call | solution.py:309
  (1 shorter events, 0.0 us)
Async XLA Ops:
  0.6 13.9 %copy-start = (bf16[4,1024,128]{2,1,0:T(8,128)(2,1)S(1)}, bf16[4,1024,128]{2,1,0:T(8,128)(2,1)}, u32[]{:S(2)}) copy-start(bf16[4,1024,128]{2,1,0:T(8,128)(2,1)} %keys_ref.1) | copy-start | bytes 3145732
  0.6 13.9 %copy-start.1 = (bf16[4,1024,128]{2,1,0:T(8,128)(2,1)S(1)}, bf16[4,1024,128]{2,1,0:T(8,128)(2,1)}, u32[]{:S(2)}) copy-start(bf16[4,1024,128]{2,1,0:T(8,128)(2,1)} %values_ref.1) | copy-start | bytes 3145732
  2.2 21.0 %collective-permute-start = (bf16[64,2048]{1,0:T(8,128)(2,1)S(1)}, bf16[64,2048]{1,0:T(8,128)(2,1)S(1)}, u32[]{:S(2)}, u32[]{:S(2)}) collective-permute-start(bf16[64,2048]{1,0:T(8,128)(2,1)S(1)} %get-tuple-element.22), channel_id=1, source_target_pairs={{0,1},{1,0},{2,3},{3,2},{4,5},{5,4},{6,7},{7,6},{8,9},{9,8},{10,11... | collective-permute-start | bytes 786440 | tf_op jit(solution)/shard_map/ppermute | solution.py:215
  45.1 6.7 %collective-permute-start.1 = (bf16[4,512]{1,0:T(4,128)(2,1)S(1)}, bf16[4,512]{1,0:T(4,128)(2,1)S(1)}, u32[]{:S(2)}, u32[]{:S(2)}) collective-permute-start(bf16[4,512]{1,0:T(4,128)(2,1)S(1)} %add_convert_fusion), channel_id=1, source_target_pairs={{0,64},{64,128},{128,192},{192,256},{256,320},{320,384},{384,448},... | collective-permute-start | bytes 12296 | tf_op jit(solution)/shard_map/ppermute | solution.py:215
